TPU v7x, 32 devices: a whole 2x2x4 slice. The times are simulated.
32 devices in a mesh: tm: 8 (over z, x), wall: 4 (over y, core).
Axes of the slice: x: 2, y: 2, z: 4, core: 2. Of those that a mesh axis runs over, the one named last changes fastest.
Arguments:
- start_state: float32 [8, 3, 384, 512], P('tm', None, 'wall'), may hold values from -6 to 6
- end_state: float32 [8, 3, 384, 512], P('tm', None, None, 'wall'), may hold values from -6 to 6
- coupling: float32 [8, 3, 384, 512], P('tm', None, None, 'wall'), may hold values from 0.5 to 1.5
- inverse_ops: float32 [8, 384, 384], P('wall')
- mirror_rows: int32 [384], replicated, may hold values from 0 to 383, as said below
- slab_steps: int32 [8], P('tm'), may hold values from 1 to 8, as said below
Outputs:
- gradient: float32 [8, 3, 384, 512], P('tm', None, 'wall')
Inputs may be any that keep to these rules, and one draw needn't show every extreme that they name: mirror_rows is an involution that maps each row of block b = y // 96 to a row of block 3 - b. `slab_steps`: some slab takes 8 steps.
All inputs are finite; a program needn't handle non-finite values.
Results may differ from a plain program's by a relative error of at most 0.00028.
Values sent between devices are 32-bit elements; how exact they have to be, the bound alone decides.
No kernel may reach another device: no remote copies, remote signals or barrier semaphores. Data moves between devices by JAX's collectives and lax.ppermute only.
A program may use at most 64 MiB of HBM per device.

v0:
```python
import jax
import jax.numpy as jnp
from jax import lax
from jax.sharding import PartitionSpec as P

STEPS_MAX = 8


def shifted(value, axis, steps):
    count = lax.axis_size(axis)
    pairs = [(source, (source + steps) % count) for source in range(count)]
    return lax.ppermute(value, axis, pairs)


def mirror(values, mirror_rows):
    parity = jnp.array([1.0, -1.0, 1.0], jnp.float32).reshape(1, 3, 1, 1)
    return jnp.take(values, mirror_rows, axis=2) * parity


def helmholtz(values, inverse_ops):
    slab_count, components, row_count, col_count = values.shape
    groups = inverse_ops.shape[0]
    blocked = values.reshape(slab_count, components, row_count, groups, col_count // groups)
    product = jnp.einsum("gyz,sczgm->scygm", inverse_ops, blocked, precision=lax.Precision.HIGHEST)
    return product.reshape(values.shape)


def adjoint(mismatch, coupling, inverse_ops, slab_steps):
    step_count = slab_steps[0]
    adjoint_state = mismatch
    for position in range(STEPS_MAX):
        advanced = helmholtz(coupling * adjoint_state, inverse_ops)
        adjoint_state = jnp.where(position < step_count, advanced, adjoint_state)
    return adjoint_state


def on_device(start_state, end_state, coupling, inverse_ops, mirror_rows, slab_steps):
    following = shifted(start_state, "tm", -1)
    following_modes = lax.all_to_all(following, "wall", split_axis=3, concat_axis=2, tiled=True)
    mismatch = end_state - mirror(following_modes, mirror_rows)
    adjoint_state = adjoint(mismatch, coupling, inverse_ops, slab_steps)
    earlier = shifted(mirror(mismatch, mirror_rows), "tm", 1)
    gradient_modes = adjoint_state - earlier
    gradient = lax.all_to_all(gradient_modes, "wall", split_axis=2, concat_axis=3, tiled=True)
    return gradient


def solution(mesh):
    in_specs = (
        P("tm", None, "wall", None),
        P("tm", None, None, "wall"),
        P("tm", None, None, "wall"),
        P("wall", None, None),
        P(),
        P("tm"),
    )
    out_specs = P("tm", None, "wall", None)
    return jax.shard_map(
        on_device, mesh=mesh, in_specs=in_specs, out_specs=out_specs, check_vma=False
    )
```

profile of v0, /device:TPU:0, one launch (start us, length us, event | category | flops | bytes accessed | tf_op | source)
XLA Modules:
  0.0 95.4 jit_solution(3559564442923137276)
XLA Ops:
  0.0 0.0 copy-start
  0.0 6.0 %collective-permute-start = (f32[1,3,96,512]{3,2,1,0:T(8,128)}, f32[1,3,96,512]{3,2,1,0:T(8,128)S(1)}, u32[]{:S(2)}, u32[]{:S(2)}) collective-permute-start(f32[1,3,96,512]{3,2,1,0:T(8,128)} %param.10), channel_id=1, source_target_pairs={{0,28},{4,0},{8,4},{12,8},{16,12},{20,16},{24,20},{28,24},{1,29},{... | collective-permute-start | bytes 1769480 | tf_op jit(solution)/shard_map/ppermute | solution.py:12
  6.0 12.9 %collective-permute-done = f32[1,3,96,512]{3,2,1,0:T(8,128)S(1)} collective-permute-done((f32[1,3,96,512]{3,2,1,0:T(8,128)}, f32[1,3,96,512]{3,2,1,0:T(8,128)S(1)}, u32[]{:S(2)}, u32[]{:S(2)}) %collective-permute-start) | collective-permute-done | bytes 589856 | tf_op jit(solution)/shard_map/ppermute | solution.py:12
  18.9 1.3 %copy.305 = f32[1,3,96,512]{2,1,0,3:T(4,128)} copy(f32[1,3,96,512]{3,2,1,0:T(8,128)S(1)} %collective-permute-done) | data formatting | bytes 1179648 | tf_op jit(solution)/shard_map/ppermute | solution.py:12
  20.2 0.0 copy-start.4
  20.2 3.6 %all-to-all-start = ((f32[1,3,96,512]{2,1,0,3:T(4,128)}), f32[1,3,96,512]{2,1,0,3:T(4,128)S(1)}, u32[]{:S(2)}, u32[]{:S(2)}) async-start(f32[1,3,96,512]{2,1,0,3:T(4,128)} %copy.305), calls=%async_computation | async-start | bytes 2097152 | tf_op jit(solution)/shard_map/all_to_all | solution.py:39
  23.9 0.0 copy-done.4
  24.6 13.7 %all-to-all-done = f32[1,3,96,512]{2,1,0,3:T(4,128)S(1)} async-done(((f32[1,3,96,512]{2,1,0,3:T(4,128)}), f32[1,3,96,512]{2,1,0,3:T(4,128)S(1)}, u32[]{:S(2)}, u32[]{:S(2)}) %all-to-all-start) | async-done | bytes 589856 | tf_op jit(solution)/shard_map/all_to_all | solution.py:39
  38.3 0.9 copy.306
  39.2 0.0 copy-start.1
  39.2 0.0 copy-start.5
  39.2 1.3 %copy.369 = f32[1,3,384,128]{3,1,2,0:T(4,128)} copy(f32[1,3,384,128]{3,2,1,0:T(8,128)S(1)} %bitcast.115) | data formatting | bytes 1179648 | tf_op jit(solution)/shard_map/all_to_all | solution.py:39
  40.5 2.4 %gather_fusion = f32[384,3,128]{2,1,0:T(4,128)S(1)} fusion(f32[3,384,128]{2,0,1:T(4,128)} %bitcast.103, s32[1024]{0:T(1024)S(1)} %pad_clamp_fusion), kind=kCustom, calls=%fused_computation.clone | custom fusion | bytes 1181184 | tf_op jit(solution)/shard_map/jit(_take)/gather | solution.py:17
  42.9 0.0 copy-done.1
  42.9 0.0 copy-done.5
  42.9 2.1 %fusion.26 = (f32[1,3,384,128]{3,2,1,0:T(8,128)}, f32[1,3,384,128]{3,2,1,0:T(8,128)S(1)}) fusion(f32[1,3,384,128]{3,2,1,0:T(8,128)S(1)} %copy-done.1, f32[1,3,384,128]{3,2,1,0:T(8,128)} %param.11, f32[3]{0:T(128)S(1)} %copy-done.5, f32[384,3,128]{2,1,0:T(4,128)S(1)} %gather_fusion, pred[384]{0:T(512)(128)(4,1)S(1)} %compare_and_fusion), kind=kLoop, calls=%fused_computation.50 | loop fusion | flops 589824 | bytes 2949516 | tf_op jit(solution)/shard_map/mul | solution.py:32
  45.0 1.3 %copy.342 = f32[3,384,128]{2,0,1:T(4,128)} copy(f32[3,384,128]{2,1,0:T(8,128)S(1)} %bitcast.102) | data formatting | bytes 1179648 | tf_op jit(solution)/shard_map/jit(_take)/Arg_0.3 | solution.py:17
  46.3 2.4 %gather_fusion.1 = f32[384,3,128]{2,1,0:T(4,128)S(1)} fusion(f32[3,384,128]{2,0,1:T(4,128)} %copy.342, s32[1024]{0:T(1024)S(1)} %pad_clamp_fusion), kind=kCustom, calls=%fused_computation.1.clone | custom fusion | bytes 1181184 | tf_op jit(solution)/shard_map/jit(_take)/gather | solution.py:17
  48.7 0.9 fusion.8
  49.6 0.2 collective-permute-start.1
  49.9 1.3 %copy.310 = f32[1,3,384,128]{2,3,1,0:T(8,128)S(1)} copy(f32[1,3,384,128]{3,2,1,0:T(8,128)} %get-tuple-element.12) | data formatting | bytes 1179648 | tf_op jit(solution)/shard_map/mul | solution.py:32
  51.2 0.0 copy-done
  51.2 1.5 %convolution_bitcast_fusion.7 = f32[1,3,384,2,64]{2,4,1,3,0:T(8,128)S(1)} fusion(f32[2,384,384]{2,1,0:T(8,128)S(1)} %copy-done, f32[3,384,2,64]{1,3,2,0:T(8,128)S(1)} %bitcast.116), kind=kOutput, calls=%fused_computation.9 | convolution fusion | flops 679477248 | bytes 2359296 | tf_op jit(solution)/shard_map/gyz,sczgm->scygm/dot_general | solution.py:24
  52.8 0.2 copy.313
  53.0 0.1 fusion.22
  53.1 1.1 %copy.314 = f32[1,3,384,128]{2,3,1,0:T(8,128)} copy(f32[1,3,384,128]{3,2,1,0:T(8,128)S(1)} %fusion.22) | data formatting | bytes 1179648 | tf_op jit(solution)/shard_map/mul | solution.py:32
  54.1 2.6 %convolution_bitcast_fusion.6 = f32[1,3,384,2,64]{2,4,1,3,0:T(8,128)S(1)} fusion(f32[2,384,384]{2,1,0:T(8,128)S(1)} %copy-done, f32[3,384,2,64]{1,3,2,0:T(8,128)} %bitcast.117), kind=kOutput, calls=%fused_computation.8 | convolution fusion | flops 679477248 | bytes 2359296 | tf_op jit(solution)/shard_map/gyz,sczgm->scygm/dot_general | solution.py:24
  56.8 1.1 %copy.317 = f32[1,3,384,128]{3,2,1,0:T(8,128)} copy(f32[1,3,384,128]{2,3,1,0:T(8,128)S(1)} %bitcast.106) | data formatting | bytes 1179648 | tf_op jit(solution)/shard_map/reshape | solution.py:25
  57.8 0.9 fusion.25
  58.8 1.3 %copy.318 = f32[1,3,384,128]{2,3,1,0:T(8,128)S(1)} copy(f32[1,3,384,128]{3,2,1,0:T(8,128)} %get-tuple-element.10) | data formatting | bytes 1179648 | tf_op jit(solution)/shard_map/mul | solution.py:32
  60.1 1.5 %convolution_bitcast_fusion.5 = f32[1,3,384,2,64]{2,4,1,3,0:T(8,128)S(1)} fusion(f32[2,384,384]{2,1,0:T(8,128)S(1)} %copy-done, f32[3,384,2,64]{1,3,2,0:T(8,128)S(1)} %bitcast.118), kind=kOutput, calls=%fused_computation.7 | convolution fusion | flops 679477248 | bytes 2359296 | tf_op jit(solution)/shard_map/gyz,sczgm->scygm/dot_general | solution.py:24
  61.7 0.2 copy.321
  61.9 0.1 fusion.21
  62.0 1.1 %copy.322 = f32[1,3,384,128]{2,3,1,0:T(8,128)} copy(f32[1,3,384,128]{3,2,1,0:T(8,128)S(1)} %fusion.21) | data formatting | bytes 1179648 | tf_op jit(solution)/shard_map/mul | solution.py:32
  63.0 2.6 %convolution_bitcast_fusion.4 = f32[1,3,384,2,64]{2,4,1,3,0:T(8,128)S(1)} fusion(f32[2,384,384]{2,1,0:T(8,128)S(1)} %copy-done, f32[3,384,2,64]{1,3,2,0:T(8,128)} %bitcast.119), kind=kOutput, calls=%fused_computation.6 | convolution fusion | flops 679477248 | bytes 2359296 | tf_op jit(solution)/shard_map/gyz,sczgm->scygm/dot_general | solution.py:24
  65.7 1.1 %copy.325 = f32[1,3,384,128]{3,2,1,0:T(8,128)} copy(f32[1,3,384,128]{2,3,1,0:T(8,128)S(1)} %bitcast.108) | data formatting | bytes 1179648 | tf_op jit(solution)/shard_map/reshape | solution.py:25
  66.7 0.9 fusion.24
  67.7 0.0 copy-start.2
  67.7 1.5 %copy.326 = f32[1,3,384,128]{2,3,1,0:T(8,128)S(1)} copy(f32[1,3,384,128]{3,2,1,0:T(8,128)} %get-tuple-element.8) | data formatting | bytes 1179648 | tf_op jit(solution)/shard_map/mul | solution.py:32
  69.2 1.5 %convolution_bitcast_fusion.3 = f32[1,3,384,2,64]{2,4,1,3,0:T(8,128)S(1)} fusion(f32[2,384,384]{2,1,0:T(8,128)S(1)} %copy-done, f32[3,384,2,64]{1,3,2,0:T(8,128)S(1)} %bitcast.120), kind=kOutput, calls=%fused_computation.5 | convolution fusion | flops 679477248 | bytes 2359296 | tf_op jit(solution)/shard_map/gyz,sczgm->scygm/dot_general | solution.py:24
  70.8 0.2 copy.329
  71.0 0.0 copy-done.2
  71.0 0.1 fusion.20
  71.1 0.2 copy.330
  71.3 1.5 %convolution_bitcast_fusion.2 = f32[1,3,384,2,64]{2,4,1,3,0:T(8,128)S(1)} fusion(f32[2,384,384]{2,1,0:T(8,128)S(1)} %copy-done, f32[3,384,2,64]{1,3,2,0:T(8,128)S(1)} %bitcast.121), kind=kOutput, calls=%fused_computation.4 | convolution fusion | flops 679477248 | bytes 2359296 | tf_op jit(solution)/shard_map/gyz,sczgm->scygm/dot_general | solution.py:24
  72.9 0.0 copy-start.3
  73.0 1.3 %copy.333 = f32[1,3,384,128]{3,2,1,0:T(8,128)} copy(f32[1,3,384,128]{2,3,1,0:T(8,128)S(1)} %bitcast.110) | data formatting | bytes 1179648 | tf_op jit(solution)/shard_map/reshape | solution.py:25
  74.2 0.0 copy-done.3
  74.2 0.9 fusion.23
  75.2 1.3 %copy.334 = f32[1,3,384,128]{2,3,1,0:T(8,128)S(1)} copy(f32[1,3,384,128]{3,2,1,0:T(8,128)} %get-tuple-element.6) | data formatting | bytes 1179648 | tf_op jit(solution)/shard_map/mul | solution.py:32
  76.5 1.5 %convolution_bitcast_fusion.1 = f32[1,3,384,2,64]{2,4,1,3,0:T(8,128)S(1)} fusion(f32[2,384,384]{2,1,0:T(8,128)S(1)} %copy-done, f32[3,384,2,64]{1,3,2,0:T(8,128)S(1)} %bitcast.122), kind=kOutput, calls=%fused_computation.3 | convolution fusion | flops 679477248 | bytes 2359296 | tf_op jit(solution)/shard_map/gyz,sczgm->scygm/dot_general | solution.py:24
  78.0 0.2 copy.337
  78.3 0.1 fusion.19
  78.4 0.2 copy.338
  78.6 1.5 %convolution_bitcast_fusion = f32[1,3,384,2,64]{2,4,1,3,0:T(8,128)S(1)} fusion(f32[2,384,384]{2,1,0:T(8,128)S(1)} %copy-done, f32[3,384,2,64]{1,3,2,0:T(8,128)S(1)} %bitcast.123), kind=kOutput, calls=%fused_computation.2 | convolution fusion | flops 679477248 | bytes 2359296 | tf_op jit(solution)/shard_map/gyz,sczgm->scygm/dot_general | solution.py:24
  80.2 0.2 copy.341
  80.4 0.0 collective-permute-done.1
  80.4 1.2 %select_subtract_fusion = f32[1,3,384,128]{3,2,1,0:T(8,128)S(1)} fusion(f32[1,3,384,128]{3,2,1,0:T(8,128)} %collective-permute-done.1, f32[1,3,384,128]{3,2,1,0:T(8,128)S(1)} %copy.341, pred[]{:T(512)} %bitcast, f32[1,3,384,128]{3,2,1,0:T(8,128)S(1)} %copy.337, f32[1,3,384,128]{3,2,1,0:T(8,128)S(1)} %get-tuple-element.7, pred[]{:T(512)} %bitcast.1), kind=kLoop, calls=%fused_computation.32 | loop fusion | flops 442368 | bytes 2949122 | tf_op jit(solution)/shard_map/sub | solution.py:43
  81.6 0.6 copy.344
  82.2 11.9 %all_to_all.36 = f32[1,3,384,128]{3,0,1,2:T(1,128)S(1)} all-to-all(f32[1,3,384,128]{3,0,1,2:T(1,128)S(1)} %copy.344), channel_id=1, replica_groups=mesh['tm'=8,'wall'=4] {'wall'}, dimensions={2} | all-to-all | bytes 1179648 | tf_op jit(solution)/shard_map/all_to_all | solution.py:44
  94.2 0.4 copy.346
  94.6 0.9 copy.347
  (13 shorter events, 0.4 us)
Async XLA Ops:
  0.0 51.2 %copy-start = (f32[2,384,384]{2,1,0:T(8,128)S(1)}, f32[2,384,384]{2,1,0:T(8,128)}, u32[]{:S(2)}) copy-start(f32[2,384,384]{2,1,0:T(8,128)} %param.13) | copy-start | bytes 3538948
  0.0 18.9 %collective-permute-start = (f32[1,3,96,512]{3,2,1,0:T(8,128)}, f32[1,3,96,512]{3,2,1,0:T(8,128)S(1)}, u32[]{:S(2)}, u32[]{:S(2)}) collective-permute-start(f32[1,3,96,512]{3,2,1,0:T(8,128)} %param.10), channel_id=1, source_target_pairs={{0,28},{4,0},{8,4},{12,8},{16,12},{20,16},{24,20},{28,24},{1,29},{... | collective-permute-start | bytes 1769480 | tf_op jit(solution)/shard_map/ppermute | solution.py:12
  20.2 3.7 %copy-start.4 = (s32[384]{0:T(512)S(1)}, s32[384]{0:T(512)}, u32[]{:S(2)}) copy-start(s32[384]{0:T(512)} %param.14) | copy-start | bytes 4612
  20.2 18.1 %all-to-all-start = ((f32[1,3,96,512]{2,1,0,3:T(4,128)}), f32[1,3,96,512]{2,1,0,3:T(4,128)S(1)}, u32[]{:S(2)}, u32[]{:S(2)}) async-start(f32[1,3,96,512]{2,1,0,3:T(4,128)} %copy.305), calls=%async_computation | async-start | bytes 2097152 | tf_op jit(solution)/shard_map/all_to_all | solution.py:39
  39.2 3.7 %copy-start.1 = (f32[1,3,384,128]{3,2,1,0:T(8,128)S(1)}, f32[1,3,384,128]{3,2,1,0:T(8,128)}, u32[]{:S(2)}) copy-start(f32[1,3,384,128]{3,2,1,0:T(8,128)} %param.12) | copy-start | bytes 1769476
  39.2 3.7 %copy-start.5 = (f32[3]{0:T(128)S(1)}, f32[3]{0:T(128)}, u32[]{:S(2)}) copy-start(f32[3]{0:T(128)} %constant.36.clone) | copy-start | bytes 40
  49.6 30.8 %collective-permute-start.1 = (f32[1,3,384,128]{3,2,1,0:T(8,128)}, f32[1,3,384,128]{3,2,1,0:T(8,128)}, u32[]{:S(2)}, u32[]{:S(2)}) collective-permute-start(f32[1,3,384,128]{3,2,1,0:T(8,128)} %fusion.8), channel_id=1, source_target_pairs={{0,4},{4,8},{8,12},{12,16},{16,20},{20,24},{24,28},{28,0},{1,5},{5... | collective-permute-start | bytes 1769480 | tf_op jit(solution)/shard_map/ppermute | solution.py:12
  67.7 3.3 %copy-start.2 = (f32[1,3,384,128]{3,2,1,0:T(8,128)}, f32[1,3,384,128]{3,2,1,0:T(8,128)S(1)}, u32[]{:S(2)}) copy-start(f32[1,3,384,128]{3,2,1,0:T(8,128)S(1)} %get-tuple-element.9) | copy-start | bytes 1769476
  72.9 1.3 %copy-start.3 = (f32[1,3,384,128]{3,2,1,0:T(8,128)S(1)}, f32[1,3,384,128]{3,2,1,0:T(8,128)}, u32[]{:S(2)}) copy-start(f32[1,3,384,128]{3,2,1,0:T(8,128)} %copy-done.2) | copy-start | bytes 1769476
where the time goes:
time: 97.2 us; the launch traced here: 95.4 us
  waiting for transfers between devices  26.6 us (27%)
  local copies, waits for them, and re-layouts  24.2 us (25%)
  matrix products  14.4 us (15%)
  blocking collectives  11.9 us (12%)
  starting transfers between devices  9.86 us (10%)
  other arithmetic  7.32 us (8%)
  between operations  1.04 us (1%)
    dot_general x8, matrix products, helmholtz(): jnp.einsum('gyz,sczgm->scygm', inverse_ops, blocked, precision=lax.Precis...  14.4 us
    all_to_all x1, waiting for transfers between devices, on_device(): lax.all_to_all(following, 'wall', split_axis=3, concat_axis=2, tiled=True)  13.7 us
    ppermute x2, waiting for transfers between devices, shifted(): return lax.ppermute(value, axis, pairs)  12.9 us
    all_to_all x1, blocking collectives, on_device(): lax.all_to_all(gradient_modes, 'wall', split_axis=2, concat_axis=3, tiled...  11.9 us
    mul x8, local copies, waits for them, and re-layouts, adjoint(): advanced = helmholtz(coupling * adjoint_state, inverse_ops)  7.94 us
    ppermute x2, starting transfers between devices, shifted(): return lax.ppermute(value, axis, pairs)  6.21 us
    mul x8, other arithmetic, adjoint(): advanced = helmholtz(coupling * adjoint_state, inverse_ops)  5.19 us
    gather x2, local copies, waits for them, and re-layouts, mirror(): return jnp.take(values, mirror_rows, axis=2) * parity  4.78 us
  transfers between devices with their start and end apart: 3, of which 2 were waited for; matrix products, arithmetic and copies ran while one was open for 32% of the time, Pallas kernels for 0%

commit v1 on v0

v1 whole, which is shorter than its diff:
```python
import functools

import jax
import jax.numpy as jnp
from jax import lax
from jax.experimental import pallas as pl
from jax.experimental.pallas import tpu as pltpu
from jax.sharding import PartitionSpec as P

STEPS_MAX = 8
LANES = 128
HALF = LANES // 2


def split(values):
    high = values.astype(jnp.bfloat16)
    low = (values - high.astype(jnp.float32)).astype(jnp.bfloat16)
    return high, low


def swap_halves(values):
    return pltpu.roll(values, HALF, 1)


def left_half(shape):
    return lax.broadcasted_iota(jnp.int32, shape, 1) < HALF


def to_groups(first, second):
    left = left_half(first.shape)
    return jnp.where(left, first, swap_halves(second)), jnp.where(left, swap_halves(first), second)


def mirror_block(pieces, mirror_ref, block, rows, count):
    partner = count - 1 - block
    target = mirror_ref[block] - partner * rows
    lane = lax.broadcasted_iota(jnp.int32, (rows, rows), 0)
    one_hot = (lane == target).astype(jnp.bfloat16)
    values = jnp.concatenate(pieces, axis=1)
    high, low = split(values)
    return jnp.dot(
        jnp.concatenate([one_hot, one_hot], axis=1),
        jnp.concatenate([high, low], axis=0),
        preferred_element_type=jnp.float32,
    )


def prepare_kernel(count, rows, wall_ref, mirror_ref, end_ref, ops_ref, *outs):
    wall = wall_ref[0]
    ops_out, sends = outs[0], outs[1:]
    ny = ops_ref.shape[1]
    for group in range(2):
        high, low = split(ops_ref[group])
        ops_out[group, :, 0:ny] = high
        ops_out[group, :, ny : 2 * ny] = high
        ops_out[group, :, 2 * ny : 3 * ny] = low
    for step in range(count):
        source = count - 1 - (wall ^ step)
        at = pl.ds(pl.multiple_of(source * rows, 8), rows)
        moved = mirror_block([end_ref[c, at, :] for c in range(3)], mirror_ref, source, rows, count)
        for c, sign in enumerate((1.0, -1.0, 1.0)):
            sends[step][c] = sign * moved[:, c * LANES : (c + 1) * LANES]


def adjoint_kernel(count, rows, wall_ref, steps_ref, mirror_ref, end_ref, coupling_ref, ops_ref, *rest):
    pieces, outs = rest[:count], rest[count : 2 * count]
    gains, scaled, state = rest[2 * count :]
    wall = wall_ref[0]
    ny = end_ref.shape[1]
    gains[0], gains[1] = to_groups(coupling_ref[0], coupling_ref[1])
    gains[2] = coupling_ref[2]
    for step in range(count):
        block = wall ^ step
        partner = count - 1 - block
        at = pl.ds(pl.multiple_of(partner * rows, 8), rows)
        moved = mirror_block([pieces[step][c] for c in range(3)], mirror_ref, block, rows, count)
        first = end_ref[0, at, :] - moved[:, :LANES]
        second = end_ref[1, at, :] + moved[:, LANES : 2 * LANES]
        state[0, at, :], state[1, at, :] = to_groups(first, second)
        state[2, at, :] = end_ref[2, at, :] - moved[:, 2 * LANES :]

    def advance(_, carry):
        for slot in range(3):
            high, low = split(gains[slot] * state[slot])
            scaled[slot, 0:ny] = high
            scaled[slot, ny : 2 * ny] = low
            scaled[slot, 2 * ny : 3 * ny] = high
        shared = []
        for group in range(2):
            product = jnp.dot(
                ops_ref[group],
                jnp.concatenate([scaled[group], scaled[2]], axis=1),
                preferred_element_type=jnp.float32,
            )
            state[group] = product[:, :LANES]
            shared.append(product[:, LANES:])
        state[2] = jnp.where(left_half(shared[0].shape), shared[0], shared[1])
        return carry

    lax.fori_loop(0, jnp.minimum(steps_ref[0], STEPS_MAX), advance, 0)
    for step in range(count):
        at = pl.ds(pl.multiple_of((wall ^ step) * rows, 8), rows)
        outs[step][0], outs[step][1] = to_groups(state[0, at, :], state[1, at, :])
        outs[step][2] = state[2, at, :]


def combine_kernel(count, wall_ref, start_ref, *rest):
    adjoint_parts, mirrored_parts, out_ref = rest[:count], rest[count : 2 * count], rest[2 * count]
    wall = wall_ref[0]
    for step in range(count):
        at = pl.ds(pl.multiple_of((wall ^ step) * LANES, LANES), LANES)
        out_ref[0, :, at] = adjoint_parts[step][0] - (mirrored_parts[step][0] - start_ref[0, :, at])


def send(parts, steps, shape, first_step=0):
    slabs, count = shape
    moved = []
    for step, part in enumerate(parts):
        step += first_step
        pairs = [
            (t * count + w, (t + steps) % slabs * count + (w ^ step)) for t in range(slabs) for w in range(count)
        ]
        moved.append(lax.ppermute(part, ("tm", "wall"), pairs))
    return moved


def on_device(shape, start_state, end_state, coupling, inverse_ops, mirror_rows, slab_steps):
    slabs, count = shape
    rows = start_state.shape[2]
    ny = end_state.shape[2]
    start, end, gain = start_state[0], end_state[0], coupling[0]
    wall = lax.axis_index("wall").astype(jnp.int32).reshape(1)
    mirror_blocks = mirror_rows.reshape(count, 1, rows)
    smem = pl.BlockSpec(memory_space=pltpu.SMEM)
    vmem = pl.BlockSpec(memory_space=pltpu.VMEM)
    part = jax.ShapeDtypeStruct((3, rows, LANES), jnp.float32)

    outgoing = [
        lax.dynamic_slice(start, (0, 0, (wall[0] ^ step) * LANES), (3, rows, LANES)) for step in range(count)
    ]
    incoming = send(outgoing, -1, shape)

    ops, *mirrored = pl.pallas_call(
        functools.partial(prepare_kernel, count, rows),
        out_shape=[jax.ShapeDtypeStruct((2, ny, 3 * ny), jnp.bfloat16)] + [part] * count,
        in_specs=[smem, vmem, vmem, vmem],
        out_specs=[vmem] * (1 + count),
        compiler_params=pltpu.CompilerParams(vmem_limit_bytes=24 << 20),
        cost_estimate=pl.CostEstimate(flops=10**8, bytes_accessed=4 << 20, transcendentals=0),
        name="prepare",
    )(wall, mirror_blocks, end, inverse_ops)

    mirrored, incoming = lax.optimization_barrier((mirrored, incoming))
    mirrored = send(mirrored, 1, shape)

    adjoint = pl.pallas_call(
        functools.partial(adjoint_kernel, count, rows),
        out_shape=[part] * count,
        in_specs=[smem, smem] + [vmem] * (4 + count),
        out_specs=[vmem] * count,
        scratch_shapes=[
            pltpu.VMEM((3, ny, LANES), jnp.float32),
            pltpu.VMEM((3, 3 * ny, LANES), jnp.bfloat16),
            pltpu.VMEM((3, ny, LANES), jnp.float32),
        ],
        compiler_params=pltpu.CompilerParams(vmem_limit_bytes=24 << 20),
        cost_estimate=pl.CostEstimate(flops=4 * 10**9, bytes_accessed=4 << 20, transcendentals=0),
        name="adjoint",
    )(wall, slab_steps, mirror_blocks, end, gain, ops, *incoming)

    returned = [adjoint[0]]
    for step in range(1, count):
        pairs = [(w, w ^ step) for w in range(count)]
        returned.append(lax.ppermute(adjoint[step], "wall", pairs))

    block = pl.BlockSpec((1, rows, LANES), lambda c: (c, 0, 0))
    whole = pl.BlockSpec((1, rows, count * LANES), lambda c: (c, 0, 0))
    gradient = pl.pallas_call(
        functools.partial(combine_kernel, count),
        grid=(3,),
        out_shape=jax.ShapeDtypeStruct(start.shape, jnp.float32),
        in_specs=[smem, whole] + [block] * (2 * count),
        out_specs=whole,
        compiler_params=pltpu.CompilerParams(vmem_limit_bytes=24 << 20),
        cost_estimate=pl.CostEstimate(flops=10**6, bytes_accessed=3 << 20, transcendentals=0),
        name="combine",
    )(wall, start, *returned, *mirrored)
    return gradient[None]


def solution(mesh):
    in_specs = (
        P("tm", None, "wall", None),
        P("tm", None, None, "wall"),
        P("tm", None, None, "wall"),
        P("wall", None, None),
        P(),
        P("tm"),
    )
    out_specs = P("tm", None, "wall", None)
    shape = (mesh.shape["tm"], mesh.shape["wall"])
    return jax.shard_map(
        functools.partial(on_device, shape),
        mesh=mesh,
        in_specs=in_specs,
        out_specs=out_specs,
        check_vma=False,
    )
```

time: 97.2 us -> 46.4 us (0.48); the launches traced: 95.4 us -> 45.8 us
  local copies, waits for them, and re-layouts: 24.2 us -> 3.1 us
  matrix products: 14.4 us -> 0 us
  blocking collectives: 11.9 us -> 0 us
  starting transfers between devices: 9.86 us -> 19.7 us
  waiting for transfers between devices: 26.6 us -> 18.1 us
  other arithmetic: 7.32 us -> 0 us
  Pallas kernels: 0 us -> 4.17 us
    dot_general x8 -> x0, matrix products: 14.4 us -> none  [helmholtz(): jnp.einsum('gyz,sczgm->scygm', inverse_ops, blocked, precision=lax.Precis...]
    all_to_all x1 -> x0, waiting for transfers between devices: 13.7 us -> none  [on_device(): lax.all_to_all(following, 'wall', split_axis=3, concat_axis=2, tiled=True)]
    ppermute x2 -> x11, starting transfers between devices: 6.21 us -> 19.7 us  [the longest x8 17.7 us: send(): moved.append(lax.ppermute(part, ('tm', 'wall'), pairs))]
    all_to_all x1 -> x0, blocking collectives: 11.9 us -> none  [on_device(): lax.all_to_all(gradient_modes, 'wall', split_axis=2, concat_axis=3, tiled...]
    mul x8 -> x0, local copies, waits for them, and re-layouts: 7.94 us -> none  [adjoint(): advanced = helmholtz(coupling * adjoint_state, inverse_ops)]
    mul x9 -> x0, other arithmetic: 6.13 us -> none  [the longest x8 5.19 us: adjoint(): advanced = helmholtz(coupling * adjoint_state, inverse_ops)]
    ppermute x2 -> x11, waiting for transfers between devices: 12.9 us -> 18.1 us  [the longest x8 18.1 us: send(): moved.append(lax.ppermute(part, ('tm', 'wall'), pairs))]
    gather x2 -> x0, local copies, waits for them, and re-layouts: 4.78 us -> none  [mirror(): return jnp.take(values, mirror_rows, axis=2) * parity]
  transfers between devices with their start and end apart: 3 -> 11, of which waited for: 2 -> 7; matrix products, arithmetic and copies ran while one was open for 32% -> 2% of each run, Pallas kernels for 0% -> 1%
where the time goes in v1:
time: 46.4 us; the launch traced here: 45.8 us
  starting transfers between devices  19.7 us (42%)
  waiting for transfers between devices  18.1 us (39%)
  Pallas kernels  4.17 us (9%)
  local copies, waits for them, and re-layouts  3.1 us (7%)
  between operations  0.7 us (2%)
    ppermute x8, waiting for transfers between devices, send(): moved.append(lax.ppermute(part, ('tm', 'wall'), pairs))  18.1 us
    ppermute x8, starting transfers between devices, send(): moved.append(lax.ppermute(part, ('tm', 'wall'), pairs))  17.7 us
    pallas_call x1, Pallas kernels, on_device(): pl.pallas_call(functools.partial(adjoint_kernel, count, rows), out_shape=...  2.09 us
    ppermute x3, starting transfers between devices, on_device(): returned.append(lax.ppermute(adjoint[step], 'wall', pairs))  1.94 us
    pallas_call x1, Pallas kernels, on_device(): pl.pallas_call(functools.partial(combine_kernel, count), grid=(3,), out_s...  1.48 us
    dynamic_slice x1, local copies, waits for them, and re-layouts, on_device(): lax.dynamic_slice(start, (0, 0, (wall[0] ^ step) * LANES), (3, rows, LANES))  1.27 us
    unnamed x8, local copies, waits for them, and re-layouts  1.07 us
  transfers between devices with their start and end apart: 11, of which 7 were waited for; matrix products, arithmetic and copies ran while one was open for 2% of the time, Pallas kernels for 1%

profile of v1, /device:TPU:0, one launch (start us, length us, event | category | flops | bytes accessed | tf_op | source)
XLA Modules:
  0.0 45.8 jit_solution(8919461005783536895)
XLA Ops:
  0.0 0.0 copy-start.1
  0.0 1.3 %dynamic-slice_bitcast_fusion = (f32[3,96,128]{2,1,0:T(8,128)S(1)}, f32[3,96,128]{2,1,0:T(8,128)S(1)}, f32[3,96,128]{2,1,0:T(8,128)S(1)}, f32[3,96,128]{2,1,0:T(8,128)S(1)}) fusion(f32[1,3,96,512]{3,2,1,0:T(8,128)} %param.6, s32[]{:T(128)S(6)} %select_n.15, s32[]{:T(128)S(6)} %select_n.13, s32[]{:T(128)S(6)} %select_n.12, s32[]{:T(128)S(6)} %select_n.14), kind=kLoop, calls=%fused_computation | loop fusion | bytes 1179664 | tf_op jit(solution)/shard_map/dynamic_slice | solution.py:139
  1.3 6.4 %collective-permute-start.3 = (f32[3,96,128]{2,1,0:T(8,128)S(1)}, f32[3,96,128]{2,1,0:T(8,128)S(1)}, u32[]{:S(2)}, u32[]{:S(2)}) collective-permute-start(f32[3,96,128]{2,1,0:T(8,128)S(1)} %get-tuple-element.39), channel_id=1, source_target_pairs={{0,31},{1,30},{2,29},{3,28},{4,3},{5,2},{6,1},{7,0},{8,7},{9,6},{1... | collective-permute-start | bytes 442376 | tf_op jit(solution)/shard_map/ppermute | solution.py:123
  7.7 0.8 %collective-permute-start.1 = (f32[3,96,128]{2,1,0:T(8,128)S(1)}, f32[3,96,128]{2,1,0:T(8,128)S(1)}, u32[]{:S(2)}, u32[]{:S(2)}) collective-permute-start(f32[3,96,128]{2,1,0:T(8,128)S(1)} %get-tuple-element.40), channel_id=1, source_target_pairs={{0,29},{1,28},{2,31},{3,30},{4,1},{5,0},{6,3},{7,2},{8,5},{9,4},{1... | collective-permute-start | bytes 442376 | tf_op jit(solution)/shard_map/ppermute | solution.py:123
  8.5 1.4 %collective-permute-start = (f32[3,96,128]{2,1,0:T(8,128)S(1)}, f32[3,96,128]{2,1,0:T(8,128)S(1)}, u32[]{:S(2)}, u32[]{:S(2)}) collective-permute-start(f32[3,96,128]{2,1,0:T(8,128)S(1)} %get-tuple-element.41), channel_id=1, source_target_pairs={{0,28},{1,29},{2,30},{3,31},{4,0},{5,1},{6,2},{7,3},{8,4},{9,5},{1... | collective-permute-start | bytes 442376 | tf_op jit(solution)/shard_map/ppermute | solution.py:123
  9.9 0.5 %collective-permute-start.2 = (f32[3,96,128]{2,1,0:T(8,128)S(1)}, f32[3,96,128]{2,1,0:T(8,128)S(1)}, u32[]{:S(2)}, u32[]{:S(2)}) collective-permute-start(f32[3,96,128]{2,1,0:T(8,128)S(1)} %get-tuple-element.42), channel_id=1, source_target_pairs={{0,30},{1,31},{2,28},{3,29},{4,2},{5,3},{6,0},{7,1},{8,6},{9,7},{1... | collective-permute-start | bytes 442376 | tf_op jit(solution)/shard_map/ppermute | solution.py:123
  11.0 0.8 %reshape.11.mirror_ref = s32[4,1,96]{2,1,0:T(1,128)S(1)} reshape(s32[384]{0:T(512)} %param.10) | data formatting | bytes 3072 | tf_op jit(solution)/shard_map/reshape | solution.py:133
  11.8 0.0 copy-done.1
  11.8 0.0 copy-start.2
  11.8 1.1 %copy-done.2 = f32[1,3,384,128]{3,2,1,0:T(8,128)S(1)} copy-done((f32[1,3,384,128]{3,2,1,0:T(8,128)S(1)}, f32[1,3,384,128]{3,2,1,0:T(8,128)}, u32[]{:S(2)}) %copy-start.2) | copy-done | bytes 589848
  12.9 0.0 copy-start.3
  12.9 0.6 %prepare.1 = (bf16[2,384,1152]{2,1,0:T(8,128)(2,1)S(1)}, f32[3,96,128]{2,1,0:T(8,128)S(1)}, f32[3,96,128]{2,1,0:T(8,128)S(1)}, f32[3,96,128]{2,1,0:T(8,128)S(1)}, f32[3,96,128]{2,1,0:T(8,128)S(1)}) custom-call(s32[1]{0:T(128)} %bitcast.wall_ref, s32[4,1,96]{2,1,0:T(1,128)S(1)} %reshape.11.mirror_ref, f32[3,384,128]{2,1,0:T(8,128)S(1)} %bitcast.14, ...), custom_call_target="tpu_custom_call" | custom-call | flops 100000000 | bytes 4194304 | tf_op jit(solution)/shard_map/prepare/pallas_call | solution.py:143
  13.5 0.0 collective-permute-done.3.rest_3_
  13.5 1.6 %collective-permute-done.1.rest_1_ = f32[3,96,128]{2,1,0:T(8,128)S(1)} collective-permute-done((f32[3,96,128]{2,1,0:T(8,128)S(1)}, f32[3,96,128]{2,1,0:T(8,128)S(1)}, u32[]{:S(2)}, u32[]{:S(2)}) %collective-permute-start.1) | collective-permute-done | bytes 147488 | tf_op jit(solution)/shard_map/ppermute | solution.py:123
  15.1 3.2 %collective-permute-done.rest_0_ = f32[3,96,128]{2,1,0:T(8,128)S(1)} collective-permute-done((f32[3,96,128]{2,1,0:T(8,128)S(1)}, f32[3,96,128]{2,1,0:T(8,128)S(1)}, u32[]{:S(2)}, u32[]{:S(2)}) %collective-permute-start) | collective-permute-done | bytes 147488 | tf_op jit(solution)/shard_map/ppermute | solution.py:123
  18.3 3.2 %collective-permute-done.2.rest_2_ = f32[3,96,128]{2,1,0:T(8,128)S(1)} collective-permute-done((f32[3,96,128]{2,1,0:T(8,128)S(1)}, f32[3,96,128]{2,1,0:T(8,128)S(1)}, u32[]{:S(2)}, u32[]{:S(2)}) %collective-permute-start.2) | collective-permute-done | bytes 147488 | tf_op jit(solution)/shard_map/ppermute | solution.py:123
  21.4 0.0 copy-done.3
  21.4 0.0 copy-start
  21.4 2.1 %adjoint.1 = (f32[3,96,128]{2,1,0:T(8,128)S(1)}, f32[3,96,128]{2,1,0:T(8,128)S(1)}, f32[3,96,128]{2,1,0:T(8,128)S(1)}, f32[3,96,128]{2,1,0:T(8,128)S(1)}) custom-call(s32[1]{0:T(128)} %bitcast.wall_ref, s32[1]{0:T(128)S(6)} %copy.7.steps_ref, s32[4,1,96]{2,1,0:T(1,128)S(1)} %reshape.11.mirror_ref, f32[3,384,128]{2,1,0:T(8,128)S(1)} %bitcast.15, ...), custom_call_target="tpu_custom_call" | custom-call | flops 4000000000 | bytes 4194304 | tf_op jit(solution)/shard_map/adjoint/pallas_call | solution.py:156
  23.5 0.2 collective-permute-start.4
  23.7 0.5 %collective-permute-start.5 = (f32[3,96,128]{2,1,0:T(8,128)S(1)}, f32[3,96,128]{2,1,0:T(8,128)S(1)}, u32[]{:S(2)}, u32[]{:S(2)}) collective-permute-start(f32[3,96,128]{2,1,0:T(8,128)S(1)} %get-tuple-element.33), channel_id=1, source_target_pairs={{0,2},{1,3},{2,0},{3,1},{4,6},{5,7},{6,4},{7,5},{8,10},{9,11},{10,... | collective-permute-start | bytes 442376 | tf_op jit(solution)/shard_map/ppermute | solution.py:174
  24.2 1.3 %collective-permute-start.6 = (f32[3,96,128]{2,1,0:T(8,128)S(1)}, f32[3,96,128]{2,1,0:T(8,128)S(1)}, u32[]{:S(2)}, u32[]{:S(2)}) collective-permute-start(f32[3,96,128]{2,1,0:T(8,128)S(1)} %get-tuple-element.34), channel_id=1, source_target_pairs={{0,3},{1,2},{2,1},{3,0},{4,7},{5,6},{6,5},{7,4},{8,11},{9,10},{10,... | collective-permute-start | bytes 442376 | tf_op jit(solution)/shard_map/ppermute | solution.py:174
  25.5 0.3 collective-permute-start.7
  25.8 0.0 collective-permute-start.8
  25.8 0.0 collective-permute-done.4.rest_1_
  25.8 8.2 %collective-permute-start.9 = (f32[3,96,128]{2,1,0:T(8,128)S(1)}, f32[3,96,128]{2,1,0:T(8,128)S(1)}, u32[]{:S(2)}, u32[]{:S(2)}) collective-permute-start(f32[3,96,128]{2,1,0:T(8,128)S(1)} %get-tuple-element.37), channel_id=1, source_target_pairs={{0,6},{1,7},{2,4},{3,5},{4,10},{5,11},{6,8},{7,9},{8,14},{9,15},{1... | collective-permute-start | bytes 442376 | tf_op jit(solution)/shard_map/ppermute | solution.py:123
  34.0 0.0 collective-permute-done.5.rest_2_
  34.0 0.1 collective-permute-start.10
  34.1 0.0 collective-permute-done.6.rest_3_
  34.1 0.7 %collective-permute-done.7.rest_4_ = f32[3,96,128]{2,1,0:T(8,128)S(1)} collective-permute-done((f32[3,96,128]{2,1,0:T(8,128)S(1)}, f32[3,96,128]{2,1,0:T(8,128)S(1)}, u32[]{:S(2)}, u32[]{:S(2)}) %collective-permute-start.7) | collective-permute-done | bytes 147488 | tf_op jit(solution)/shard_map/ppermute | solution.py:123
  34.8 2.0 %collective-permute-done.8.rest_5_ = f32[3,96,128]{2,1,0:T(8,128)S(1)} collective-permute-done((f32[3,96,128]{2,1,0:T(8,128)S(1)}, f32[3,96,128]{2,1,0:T(8,128)S(1)}, u32[]{:S(2)}, u32[]{:S(2)}) %collective-permute-start.8) | collective-permute-done | bytes 147488 | tf_op jit(solution)/shard_map/ppermute | solution.py:123
  36.9 4.9 %collective-permute-done.9.rest_6_ = f32[3,96,128]{2,1,0:T(8,128)S(1)} collective-permute-done((f32[3,96,128]{2,1,0:T(8,128)S(1)}, f32[3,96,128]{2,1,0:T(8,128)S(1)}, u32[]{:S(2)}, u32[]{:S(2)}) %collective-permute-start.9) | collective-permute-done | bytes 147488 | tf_op jit(solution)/shard_map/ppermute | solution.py:123
  41.8 2.5 %collective-permute-done.10.rest_7_ = f32[3,96,128]{2,1,0:T(8,128)S(1)} collective-permute-done((f32[3,96,128]{2,1,0:T(8,128)S(1)}, f32[3,96,128]{2,1,0:T(8,128)S(1)}, u32[]{:S(2)}, u32[]{:S(2)}) %collective-permute-start.10) | collective-permute-done | bytes 147488 | tf_op jit(solution)/shard_map/ppermute | solution.py:123
  44.3 0.0 copy-done
  44.3 1.5 %combine.1 = f32[3,96,512]{2,1,0:T(8,128)} custom-call(s32[1]{0:T(128)} %bitcast.wall_ref, f32[3,96,512]{2,1,0:T(8,128)S(1)} %bitcast.13, f32[3,96,128]{2,1,0:T(8,128)S(1)} %get-tuple-element.31.rest_0_, f32[3,96,128]{2,1,0:T(8,128)S(1)} %collective-permute-done.4.rest_1_, f32[3,96,128]{2,1,0:T(8,128)S(1)} %collective-permute-done.5.rest_2_, ...), custom_call_target="tpu_custom_call" | custom-call | flops 1000000 | bytes 3145728 | tf_op jit(solution)/shard_map/combine/pallas_call | solution.py:178
Async XLA Ops:
  0.0 11.8 %copy-start.1 = (f32[2,384,384]{2,1,0:T(8,128)S(1)}, f32[2,384,384]{2,1,0:T(8,128)}, u32[]{:S(2)}) copy-start(f32[2,384,384]{2,1,0:T(8,128)} %ops_ref.1) | copy-start | bytes 3538948
  1.3 12.2 %collective-permute-start.3 = (f32[3,96,128]{2,1,0:T(8,128)S(1)}, f32[3,96,128]{2,1,0:T(8,128)S(1)}, u32[]{:S(2)}, u32[]{:S(2)}) collective-permute-start(f32[3,96,128]{2,1,0:T(8,128)S(1)} %get-tuple-element.39), channel_id=1, source_target_pairs={{0,31},{1,30},{2,29},{3,28},{4,3},{5,2},{6,1},{7,0},{8,7},{9,6},{1... | collective-permute-start | bytes 442376 | tf_op jit(solution)/shard_map/ppermute | solution.py:123
  7.7 7.4 %collective-permute-start.1 = (f32[3,96,128]{2,1,0:T(8,128)S(1)}, f32[3,96,128]{2,1,0:T(8,128)S(1)}, u32[]{:S(2)}, u32[]{:S(2)}) collective-permute-start(f32[3,96,128]{2,1,0:T(8,128)S(1)} %get-tuple-element.40), channel_id=1, source_target_pairs={{0,29},{1,28},{2,31},{3,30},{4,1},{5,0},{6,3},{7,2},{8,5},{9,4},{1... | collective-permute-start | bytes 442376 | tf_op jit(solution)/shard_map/ppermute | solution.py:123
  8.5 9.7 %collective-permute-start = (f32[3,96,128]{2,1,0:T(8,128)S(1)}, f32[3,96,128]{2,1,0:T(8,128)S(1)}, u32[]{:S(2)}, u32[]{:S(2)}) collective-permute-start(f32[3,96,128]{2,1,0:T(8,128)S(1)} %get-tuple-element.41), channel_id=1, source_target_pairs={{0,28},{1,29},{2,30},{3,31},{4,0},{5,1},{6,2},{7,3},{8,4},{9,5},{1... | collective-permute-start | bytes 442376 | tf_op jit(solution)/shard_map/ppermute | solution.py:123
  9.9 11.5 %collective-permute-start.2 = (f32[3,96,128]{2,1,0:T(8,128)S(1)}, f32[3,96,128]{2,1,0:T(8,128)S(1)}, u32[]{:S(2)}, u32[]{:S(2)}) collective-permute-start(f32[3,96,128]{2,1,0:T(8,128)S(1)} %get-tuple-element.42), channel_id=1, source_target_pairs={{0,30},{1,31},{2,28},{3,29},{4,2},{5,3},{6,0},{7,1},{8,6},{9,7},{1... | collective-permute-start | bytes 442376 | tf_op jit(solution)/shard_map/ppermute | solution.py:123
  11.8 1.1 %copy-start.2 = (f32[1,3,384,128]{3,2,1,0:T(8,128)S(1)}, f32[1,3,384,128]{3,2,1,0:T(8,128)}, u32[]{:S(2)}) copy-start(f32[1,3,384,128]{3,2,1,0:T(8,128)} %param.7) | copy-start | bytes 1769476
  12.9 8.6 %copy-start.3 = (f32[1,3,384,128]{3,2,1,0:T(8,128)S(1)}, f32[1,3,384,128]{3,2,1,0:T(8,128)}, u32[]{:S(2)}) copy-start(f32[1,3,384,128]{3,2,1,0:T(8,128)} %param.8) | copy-start | bytes 1769476
  21.4 22.9 %copy-start = (f32[1,3,96,512]{3,2,1,0:T(8,128)S(1)}, f32[1,3,96,512]{3,2,1,0:T(8,128)}, u32[]{:S(2)}) copy-start(f32[1,3,96,512]{3,2,1,0:T(8,128)} %param.6) | copy-start | bytes 1769476
  23.5 2.2 %collective-permute-start.4 = (f32[3,96,128]{2,1,0:T(8,128)S(1)}, f32[3,96,128]{2,1,0:T(8,128)S(1)}, u32[]{:S(2)}, u32[]{:S(2)}) collective-permute-start(f32[3,96,128]{2,1,0:T(8,128)S(1)} %get-tuple-element.32), channel_id=1, source_target_pairs={{0,1},{1,0},{2,3},{3,2},{4,5},{5,4},{6,7},{7,6},{8,9},{9,8},{10,11... | collective-permute-start | bytes 442376 | tf_op jit(solution)/shard_map/ppermute | solution.py:174
  23.7 10.3 %collective-permute-start.5 = (f32[3,96,128]{2,1,0:T(8,128)S(1)}, f32[3,96,128]{2,1,0:T(8,128)S(1)}, u32[]{:S(2)}, u32[]{:S(2)}) collective-permute-start(f32[3,96,128]{2,1,0:T(8,128)S(1)} %get-tuple-element.33), channel_id=1, source_target_pairs={{0,2},{1,3},{2,0},{3,1},{4,6},{5,7},{6,4},{7,5},{8,10},{9,11},{10,... | collective-permute-start | bytes 442376 | tf_op jit(solution)/shard_map/ppermute | solution.py:174
  24.2 9.9 %collective-permute-start.6 = (f32[3,96,128]{2,1,0:T(8,128)S(1)}, f32[3,96,128]{2,1,0:T(8,128)S(1)}, u32[]{:S(2)}, u32[]{:S(2)}) collective-permute-start(f32[3,96,128]{2,1,0:T(8,128)S(1)} %get-tuple-element.34), channel_id=1, source_target_pairs={{0,3},{1,2},{2,1},{3,0},{4,7},{5,6},{6,5},{7,4},{8,11},{9,10},{10,... | collective-permute-start | bytes 442376 | tf_op jit(solution)/shard_map/ppermute | solution.py:174
  25.5 9.4 %collective-permute-start.7 = (f32[3,96,128]{2,1,0:T(8,128)S(1)}, f32[3,96,128]{2,1,0:T(8,128)S(1)}, u32[]{:S(2)}, u32[]{:S(2)}) collective-permute-start(f32[3,96,128]{2,1,0:T(8,128)S(1)} %get-tuple-element.35), channel_id=1, source_target_pairs={{0,4},{1,5},{2,6},{3,7},{4,8},{5,9},{6,10},{7,11},{8,12},{9,13},{1... | collective-permute-start | bytes 442376 | tf_op jit(solution)/shard_map/ppermute | solution.py:123
  25.8 11.1 %collective-permute-start.8 = (f32[3,96,128]{2,1,0:T(8,128)S(1)}, f32[3,96,128]{2,1,0:T(8,128)S(1)}, u32[]{:S(2)}, u32[]{:S(2)}) collective-permute-start(f32[3,96,128]{2,1,0:T(8,128)S(1)} %get-tuple-element.36), channel_id=1, source_target_pairs={{0,5},{1,4},{2,7},{3,6},{4,9},{5,8},{6,11},{7,10},{8,13},{9,12},{1... | collective-permute-start | bytes 442376 | tf_op jit(solution)/shard_map/ppermute | solution.py:123
  25.8 16.0 %collective-permute-start.9 = (f32[3,96,128]{2,1,0:T(8,128)S(1)}, f32[3,96,128]{2,1,0:T(8,128)S(1)}, u32[]{:S(2)}, u32[]{:S(2)}) collective-permute-start(f32[3,96,128]{2,1,0:T(8,128)S(1)} %get-tuple-element.37), channel_id=1, source_target_pairs={{0,6},{1,7},{2,4},{3,5},{4,10},{5,11},{6,8},{7,9},{8,14},{9,15},{1... | collective-permute-start | bytes 442376 | tf_op jit(solution)/shard_map/ppermute | solution.py:123
  34.0 10.3 %collective-permute-start.10 = (f32[3,96,128]{2,1,0:T(8,128)S(1)}, f32[3,96,128]{2,1,0:T(8,128)S(1)}, u32[]{:S(2)}, u32[]{:S(2)}) collective-permute-start(f32[3,96,128]{2,1,0:T(8,128)S(1)} %get-tuple-element.38), channel_id=1, source_target_pairs={{0,7},{1,6},{2,5},{3,4},{4,11},{5,10},{6,9},{7,8},{8,15},{9,14},{1... | collective-permute-start | bytes 442376 | tf_op jit(solution)/shard_map/ppermute | solution.py:123

commit v2 on v1

--- a/solution.py
+++ b/solution.py
@@ -104,24 +104,26 @@
         outs[step][2] = state[2, at, :]
 
 
-def combine_kernel(count, wall_ref, start_ref, *rest):
-    adjoint_parts, mirrored_parts, out_ref = rest[:count], rest[count : 2 * count], rest[2 * count]
-    wall = wall_ref[0]
-    for step in range(count):
+def offset_kernel(count, wall_ref, start_ref, *rest):
+    parts, out_ref = rest[:-1], rest[-1]
+    wall = wall_ref[0]
+    for step, part in enumerate(parts):
         at = pl.ds(pl.multiple_of((wall ^ step) * LANES, LANES), LANES)
-        out_ref[0, :, at] = adjoint_parts[step][0] - (mirrored_parts[step][0] - start_ref[0, :, at])
-
-
-def send(parts, steps, shape, first_step=0):
+        out_ref[:, :, at] = part[...] - start_ref[:, :, at]
+
+
+def combine_kernel(count, wall_ref, offset_ref, *rest):
+    parts, out_ref = rest[:-1], rest[-1]
+    wall = wall_ref[0]
+    for step, part in enumerate(parts):
+        at = pl.ds(pl.multiple_of((wall ^ step) * LANES, LANES), LANES)
+        out_ref[:, :, at] = part[...] - offset_ref[:, :, at]
+
+
+def send(part, steps, flip, shape):
     slabs, count = shape
-    moved = []
-    for step, part in enumerate(parts):
-        step += first_step
-        pairs = [
-            (t * count + w, (t + steps) % slabs * count + (w ^ step)) for t in range(slabs) for w in range(count)
-        ]
-        moved.append(lax.ppermute(part, ("tm", "wall"), pairs))
-    return moved
+    pairs = [(t * count + w, (t + steps) % slabs * count + (w ^ flip)) for t in range(slabs) for w in range(count)]
+    return lax.ppermute(part, ("tm", "wall"), pairs)
 
 
 def on_device(shape, start_state, end_state, coupling, inverse_ops, mirror_rows, slab_steps):
@@ -138,7 +140,7 @@
     outgoing = [
         lax.dynamic_slice(start, (0, 0, (wall[0] ^ step) * LANES), (3, rows, LANES)) for step in range(count)
     ]
-    incoming = send(outgoing, -1, shape)
+    incoming = [send(part, -1, step, shape) for step, part in enumerate(outgoing)]
 
     ops, *mirrored = pl.pallas_call(
         functools.partial(prepare_kernel, count, rows),
@@ -150,8 +152,9 @@
         name="prepare",
     )(wall, mirror_blocks, end, inverse_ops)
 
-    mirrored, incoming = lax.optimization_barrier((mirrored, incoming))
-    mirrored = send(mirrored, 1, shape)
+    mirrored, arrived = lax.optimization_barrier((mirrored, incoming[:-1]))
+    incoming = arrived + incoming[-1:]
+    mirrored = [send(part, 1, i, shape) for i, part in enumerate(mirrored)]
 
     adjoint = pl.pallas_call(
         functools.partial(adjoint_kernel, count, rows),
@@ -170,21 +173,29 @@
 
     returned = [adjoint[0]]
     for step in range(1, count):
-        pairs = [(w, w ^ step) for w in range(count)]
-        returned.append(lax.ppermute(adjoint[step], "wall", pairs))
+        returned.append(send(adjoint[step], 0, step, shape))
 
     block = pl.BlockSpec((1, rows, LANES), lambda c: (c, 0, 0))
     whole = pl.BlockSpec((1, rows, count * LANES), lambda c: (c, 0, 0))
+    offset = pl.pallas_call(
+        functools.partial(offset_kernel, count),
+        out_shape=jax.ShapeDtypeStruct(start.shape, jnp.float32),
+        in_specs=[smem, vmem] + [vmem] * count,
+        out_specs=vmem,
+        compiler_params=pltpu.CompilerParams(vmem_limit_bytes=24 << 20),
+        cost_estimate=pl.CostEstimate(flops=10**6, bytes_accessed=40 << 20, transcendentals=0),
+        name="offset",
+    )(wall, start, *mirrored)
     gradient = pl.pallas_call(
         functools.partial(combine_kernel, count),
         grid=(3,),
         out_shape=jax.ShapeDtypeStruct(start.shape, jnp.float32),
-        in_specs=[smem, whole] + [block] * (2 * count),
+        in_specs=[smem, whole] + [block] * count,
         out_specs=whole,
         compiler_params=pltpu.CompilerParams(vmem_limit_bytes=24 << 20),
         cost_estimate=pl.CostEstimate(flops=10**6, bytes_accessed=3 << 20, transcendentals=0),
         name="combine",
-    )(wall, start, *returned, *mirrored)
+    )(wall, offset, *returned)
     return gradient[None]
 
 

time: 46.4 us -> 41.4 us (0.89)
  waiting for transfers between devices: 18.1 us -> 15.7 us
  starting transfers between devices: 19.7 us -> 17.6 us
  Pallas kernels: 4.17 us -> 3.49 us
    ppermute x11, waiting for transfers between devices: 18.1 us -> 15.7 us  [send(): return lax.ppermute(part, ('tm', 'wall'), pairs)]
    ppermute x11, starting transfers between devices: 19.7 us -> 17.6 us  [send(): return lax.ppermute(part, ('tm', 'wall'), pairs)]
    pallas_call x1, Pallas kernels: 2.09 us -> 1.33 us  [on_device(): pl.pallas_call(functools.partial(adjoint_kernel, count, rows), out_shape=...]
  transfers between devices with their start and end apart: 11 -> 11, of which waited for: 7 -> 6; matrix products, arithmetic and copies ran while one was open for 2% -> 2% of each run, Pallas kernels for 1% -> 5%
where the time goes in v2:
time: 41.4 us; the launch traced here: 40.6 us
  starting transfers between devices  17.6 us (43%)
  waiting for transfers between devices  15.7 us (38%)
  Pallas kernels  3.49 us (8%)
  local copies, waits for them, and re-layouts  3.1 us (7%)
  between operations  0.72 us (2%)
    ppermute x11, starting transfers between devices, send(): return lax.ppermute(part, ('tm', 'wall'), pairs)  17.6 us
    ppermute x11, waiting for transfers between devices, send(): return lax.ppermute(part, ('tm', 'wall'), pairs)  15.7 us
    pallas_call x1, Pallas kernels, on_device(): pl.pallas_call(functools.partial(combine_kernel, count), grid=(3,), out_s...  1.46 us
    pallas_call x1, Pallas kernels, on_device(): pl.pallas_call(functools.partial(adjoint_kernel, count, rows), out_shape=...  1.33 us
    dynamic_slice x1, local copies, waits for them, and re-layouts, on_device(): lax.dynamic_slice(start, (0, 0, (wall[0] ^ step) * LANES), (3, rows, LANES))  1.27 us
    unnamed x8, local copies, waits for them, and re-layouts  1.07 us
  transfers between devices with their start and end apart: 11, of which 6 were waited for; matrix products, arithmetic and copies ran while one was open for 2% of the time, Pallas kernels for 5%

profile of v2, /device:TPU:0, one launch (start us, length us, event | category | flops | bytes accessed | tf_op | source)
XLA Modules:
  0.0 40.6 jit_solution(10017626540689637848)
XLA Ops:
  0.0 0.0 copy-start.1
  0.0 1.3 %dynamic-slice_bitcast_fusion = (f32[3,96,128]{2,1,0:T(8,128)S(1)}, f32[3,96,128]{2,1,0:T(8,128)S(1)}, f32[3,96,128]{2,1,0:T(8,128)S(1)}, f32[3,96,128]{2,1,0:T(8,128)S(1)}) fusion(f32[1,3,96,512]{3,2,1,0:T(8,128)} %param.6, s32[]{:T(128)S(6)} %select_n.15, s32[]{:T(128)S(6)} %select_n.13, s32[]{:T(128)S(6)} %select_n.12, s32[]{:T(128)S(6)} %select_n.14), kind=kLoop, calls=%fused_computation | loop fusion | bytes 1179664 | tf_op jit(solution)/shard_map/dynamic_slice | solution.py:141
  1.3 6.0 %collective-permute-start = (f32[3,96,128]{2,1,0:T(8,128)S(1)}, f32[3,96,128]{2,1,0:T(8,128)S(1)}, u32[]{:S(2)}, u32[]{:S(2)}) collective-permute-start(f32[3,96,128]{2,1,0:T(8,128)S(1)} %get-tuple-element.39), channel_id=1, source_target_pairs={{0,28},{1,29},{2,30},{3,31},{4,0},{5,1},{6,2},{7,3},{8,4},{9,5},{1... | collective-permute-start | bytes 442376 | tf_op jit(solution)/shard_map/ppermute | solution.py:126
  7.3 0.0 collective-permute-start.1
  7.3 2.0 %collective-permute-start.2 = (f32[3,96,128]{2,1,0:T(8,128)S(1)}, f32[3,96,128]{2,1,0:T(8,128)S(1)}, u32[]{:S(2)}, u32[]{:S(2)}) collective-permute-start(f32[3,96,128]{2,1,0:T(8,128)S(1)} %get-tuple-element.40), channel_id=1, source_target_pairs={{0,30},{1,31},{2,28},{3,29},{4,2},{5,3},{6,0},{7,1},{8,6},{9,7},{1... | collective-permute-start | bytes 442376 | tf_op jit(solution)/shard_map/ppermute | solution.py:126
  9.3 0.8 %collective-permute-start.7 = (f32[3,96,128]{2,1,0:T(8,128)S(1)}, f32[3,96,128]{2,1,0:T(8,128)S(1)}, u32[]{:S(2)}, u32[]{:S(2)}) collective-permute-start(f32[3,96,128]{2,1,0:T(8,128)S(1)} %get-tuple-element.37), channel_id=1, source_target_pairs={{0,31},{1,30},{2,29},{3,28},{4,3},{5,2},{6,1},{7,0},{8,7},{9,6},{1... | collective-permute-start | bytes 442376 | tf_op jit(solution)/shard_map/ppermute | solution.py:126
  10.1 0.8 %reshape.11.mirror_ref = s32[4,1,96]{2,1,0:T(1,128)S(1)} reshape(s32[384]{0:T(512)} %param.10) | data formatting | bytes 3072 | tf_op jit(solution)/shard_map/reshape | solution.py:135
  11.5 0.0 copy-done.1
  11.5 0.0 copy-start.2
  11.5 1.1 %copy-done.2 = f32[1,3,384,128]{3,2,1,0:T(8,128)S(1)} copy-done((f32[1,3,384,128]{3,2,1,0:T(8,128)S(1)}, f32[1,3,384,128]{3,2,1,0:T(8,128)}, u32[]{:S(2)}) %copy-start.2) | copy-done | bytes 589848
  12.6 0.0 copy-start.3
  12.6 0.6 %prepare.1 = (bf16[2,384,1152]{2,1,0:T(8,128)(2,1)S(1)}, f32[3,96,128]{2,1,0:T(8,128)S(1)}, f32[3,96,128]{2,1,0:T(8,128)S(1)}, f32[3,96,128]{2,1,0:T(8,128)S(1)}, f32[3,96,128]{2,1,0:T(8,128)S(1)}) custom-call(s32[1]{0:T(128)} %bitcast.wall_ref, s32[4,1,96]{2,1,0:T(1,128)S(1)} %reshape.11.mirror_ref, f32[3,384,128]{2,1,0:T(8,128)S(1)} %bitcast.14, ...), custom_call_target="tpu_custom_call" | custom-call | flops 100000000 | bytes 4194304 | tf_op jit(solution)/shard_map/prepare/pallas_call | solution.py:145
  13.2 0.0 collective-permute-done.rest_0_
  13.2 1.5 %collective-permute-done.1.rest_1_ = f32[3,96,128]{2,1,0:T(8,128)S(1)} collective-permute-done((f32[3,96,128]{2,1,0:T(8,128)S(1)}, f32[3,96,128]{2,1,0:T(8,128)S(1)}, u32[]{:S(2)}, u32[]{:S(2)}) %collective-permute-start.1) | collective-permute-done | bytes 147488 | tf_op jit(solution)/shard_map/ppermute | solution.py:126
  14.7 3.2 %collective-permute-done.2.rest_2_ = f32[3,96,128]{2,1,0:T(8,128)S(1)} collective-permute-done((f32[3,96,128]{2,1,0:T(8,128)S(1)}, f32[3,96,128]{2,1,0:T(8,128)S(1)}, u32[]{:S(2)}, u32[]{:S(2)}) %collective-permute-start.2) | collective-permute-done | bytes 147488 | tf_op jit(solution)/shard_map/ppermute | solution.py:126
  17.9 1.1 %collective-permute-start.3 = (f32[3,96,128]{2,1,0:T(8,128)S(1)}, f32[3,96,128]{2,1,0:T(8,128)S(1)}, u32[]{:S(2)}, u32[]{:S(2)}) collective-permute-start(f32[3,96,128]{2,1,0:T(8,128)S(1)} %get-tuple-element.25), channel_id=1, source_target_pairs={{0,4},{1,5},{2,6},{3,7},{4,8},{5,9},{6,10},{7,11},{8,12},{9,13},{1... | collective-permute-start | bytes 442376 | tf_op jit(solution)/shard_map/ppermute | solution.py:126
  19.0 0.0 collective-permute-start.4
  19.0 0.8 %collective-permute-start.5 = (f32[3,96,128]{2,1,0:T(8,128)S(1)}, f32[3,96,128]{2,1,0:T(8,128)S(1)}, u32[]{:S(2)}, u32[]{:S(2)}) collective-permute-start(f32[3,96,128]{2,1,0:T(8,128)S(1)} %get-tuple-element.27), channel_id=1, source_target_pairs={{0,6},{1,7},{2,4},{3,5},{4,10},{5,11},{6,8},{7,9},{8,14},{9,15},{1... | collective-permute-start | bytes 442376 | tf_op jit(solution)/shard_map/ppermute | solution.py:126
  19.8 3.4 %collective-permute-start.6 = (f32[3,96,128]{2,1,0:T(8,128)S(1)}, f32[3,96,128]{2,1,0:T(8,128)S(1)}, u32[]{:S(2)}, u32[]{:S(2)}) collective-permute-start(f32[3,96,128]{2,1,0:T(8,128)S(1)} %get-tuple-element.28), channel_id=1, source_target_pairs={{0,7},{1,6},{2,5},{3,4},{4,11},{5,10},{6,9},{7,8},{8,15},{9,14},{1... | collective-permute-start | bytes 442376 | tf_op jit(solution)/shard_map/ppermute | solution.py:126
  23.2 0.0 collective-permute-done.7.rest_3_
  23.2 0.0 copy-done.3
  23.2 0.0 copy-start
  23.2 1.3 %adjoint.1 = (f32[3,96,128]{2,1,0:T(8,128)S(1)}, f32[3,96,128]{2,1,0:T(8,128)S(1)}, f32[3,96,128]{2,1,0:T(8,128)S(1)}, f32[3,96,128]{2,1,0:T(8,128)S(1)}) custom-call(s32[1]{0:T(128)} %bitcast.wall_ref, s32[1]{0:T(128)S(6)} %copy.7.steps_ref, s32[4,1,96]{2,1,0:T(1,128)S(1)} %reshape.11.mirror_ref, f32[3,384,128]{2,1,0:T(8,128)S(1)} %bitcast.15, ...), custom_call_target="tpu_custom_call" | custom-call | flops 4000000000 | bytes 4194304 | tf_op jit(solution)/shard_map/adjoint/pallas_call | solution.py:159
  24.5 0.1 collective-permute-start.8
  24.6 4.0 %collective-permute-done.3.rest_0_ = f32[3,96,128]{2,1,0:T(8,128)S(1)} collective-permute-done((f32[3,96,128]{2,1,0:T(8,128)S(1)}, f32[3,96,128]{2,1,0:T(8,128)S(1)}, u32[]{:S(2)}, u32[]{:S(2)}) %collective-permute-start.3) | collective-permute-done | bytes 147488 | tf_op jit(solution)/shard_map/ppermute | solution.py:126
  28.7 0.5 %collective-permute-start.9 = (f32[3,96,128]{2,1,0:T(8,128)S(1)}, f32[3,96,128]{2,1,0:T(8,128)S(1)}, u32[]{:S(2)}, u32[]{:S(2)}) collective-permute-start(f32[3,96,128]{2,1,0:T(8,128)S(1)} %get-tuple-element.35), channel_id=1, source_target_pairs={{0,2},{1,3},{2,0},{3,1},{4,6},{5,7},{6,4},{7,5},{8,10},{9,11},{10,... | collective-permute-start | bytes 442376 | tf_op jit(solution)/shard_map/ppermute | solution.py:126
  29.2 0.0 collective-permute-done.4.rest_1_
  29.2 2.9 %collective-permute-start.10 = (f32[3,96,128]{2,1,0:T(8,128)S(1)}, f32[3,96,128]{2,1,0:T(8,128)S(1)}, u32[]{:S(2)}, u32[]{:S(2)}) collective-permute-start(f32[3,96,128]{2,1,0:T(8,128)S(1)} %get-tuple-element.36), channel_id=1, source_target_pairs={{0,3},{1,2},{2,1},{3,0},{4,7},{5,6},{6,5},{7,4},{8,11},{9,10},{10,... | collective-permute-start | bytes 442376 | tf_op jit(solution)/shard_map/ppermute | solution.py:126
  32.1 2.0 %collective-permute-done.5.rest_2_ = f32[3,96,128]{2,1,0:T(8,128)S(1)} collective-permute-done((f32[3,96,128]{2,1,0:T(8,128)S(1)}, f32[3,96,128]{2,1,0:T(8,128)S(1)}, u32[]{:S(2)}, u32[]{:S(2)}) %collective-permute-start.5) | collective-permute-done | bytes 147488 | tf_op jit(solution)/shard_map/ppermute | solution.py:126
  34.1 0.0 collective-permute-done.6.rest_3_
  34.1 0.0 copy-done
  34.1 0.1 offset.1.offset_ref
  34.2 0.0 collective-permute-done.8.rest_1_
  34.3 4.4 %collective-permute-done.9.rest_2_ = f32[3,96,128]{2,1,0:T(8,128)S(1)} collective-permute-done((f32[3,96,128]{2,1,0:T(8,128)S(1)}, f32[3,96,128]{2,1,0:T(8,128)S(1)}, u32[]{:S(2)}, u32[]{:S(2)}) %collective-permute-start.9) | collective-permute-done | bytes 147488 | tf_op jit(solution)/shard_map/ppermute | solution.py:126
  38.7 0.5 %collective-permute-done.10.rest_3_ = f32[3,96,128]{2,1,0:T(8,128)S(1)} collective-permute-done((f32[3,96,128]{2,1,0:T(8,128)S(1)}, f32[3,96,128]{2,1,0:T(8,128)S(1)}, u32[]{:S(2)}, u32[]{:S(2)}) %collective-permute-start.10) | collective-permute-done | bytes 147488 | tf_op jit(solution)/shard_map/ppermute | solution.py:126
  39.2 1.5 %combine.1 = f32[3,96,512]{2,1,0:T(8,128)} custom-call(s32[1]{0:T(128)} %bitcast.wall_ref, f32[3,96,512]{2,1,0:T(8,128)S(1)} %offset.1.offset_ref, f32[3,96,128]{2,1,0:T(8,128)S(1)} %get-tuple-element.33.rest_0_, f32[3,96,128]{2,1,0:T(8,128)S(1)} %collective-permute-done.8.rest_1_, f32[3,96,128]{2,1,0:T(8,128)S(1)} %collective-permute-done.9.rest_2_, ...), custom_call_target="tpu_custom_call" | custom-call | flops 1000000 | bytes 3145728 | tf_op jit(solution)/shard_map/combine/pallas_call | solution.py:189
Async XLA Ops:
  0.0 11.5 %copy-start.1 = (f32[2,384,384]{2,1,0:T(8,128)S(1)}, f32[2,384,384]{2,1,0:T(8,128)}, u32[]{:S(2)}) copy-start(f32[2,384,384]{2,1,0:T(8,128)} %ops_ref.1) | copy-start | bytes 3538948
  1.3 11.9 %collective-permute-start = (f32[3,96,128]{2,1,0:T(8,128)S(1)}, f32[3,96,128]{2,1,0:T(8,128)S(1)}, u32[]{:S(2)}, u32[]{:S(2)}) collective-permute-start(f32[3,96,128]{2,1,0:T(8,128)S(1)} %get-tuple-element.39), channel_id=1, source_target_pairs={{0,28},{1,29},{2,30},{3,31},{4,0},{5,1},{6,2},{7,3},{8,4},{9,5},{1... | collective-permute-start | bytes 442376 | tf_op jit(solution)/shard_map/ppermute | solution.py:126
  7.3 7.4 %collective-permute-start.1 = (f32[3,96,128]{2,1,0:T(8,128)S(1)}, f32[3,96,128]{2,1,0:T(8,128)S(1)}, u32[]{:S(2)}, u32[]{:S(2)}) collective-permute-start(f32[3,96,128]{2,1,0:T(8,128)S(1)} %get-tuple-element.38), channel_id=1, source_target_pairs={{0,29},{1,28},{2,31},{3,30},{4,1},{5,0},{6,3},{7,2},{8,5},{9,4},{1... | collective-permute-start | bytes 442376 | tf_op jit(solution)/shard_map/ppermute | solution.py:126
  7.3 10.6 %collective-permute-start.2 = (f32[3,96,128]{2,1,0:T(8,128)S(1)}, f32[3,96,128]{2,1,0:T(8,128)S(1)}, u32[]{:S(2)}, u32[]{:S(2)}) collective-permute-start(f32[3,96,128]{2,1,0:T(8,128)S(1)} %get-tuple-element.40), channel_id=1, source_target_pairs={{0,30},{1,31},{2,28},{3,29},{4,2},{5,3},{6,0},{7,1},{8,6},{9,7},{1... | collective-permute-start | bytes 442376 | tf_op jit(solution)/shard_map/ppermute | solution.py:126
  9.3 13.9 %collective-permute-start.7 = (f32[3,96,128]{2,1,0:T(8,128)S(1)}, f32[3,96,128]{2,1,0:T(8,128)S(1)}, u32[]{:S(2)}, u32[]{:S(2)}) collective-permute-start(f32[3,96,128]{2,1,0:T(8,128)S(1)} %get-tuple-element.37), channel_id=1, source_target_pairs={{0,31},{1,30},{2,29},{3,28},{4,3},{5,2},{6,1},{7,0},{8,7},{9,6},{1... | collective-permute-start | bytes 442376 | tf_op jit(solution)/shard_map/ppermute | solution.py:126
  11.5 1.1 %copy-start.2 = (f32[1,3,384,128]{3,2,1,0:T(8,128)S(1)}, f32[1,3,384,128]{3,2,1,0:T(8,128)}, u32[]{:S(2)}) copy-start(f32[1,3,384,128]{3,2,1,0:T(8,128)} %param.7) | copy-start | bytes 1769476
  12.6 10.6 %copy-start.3 = (f32[1,3,384,128]{3,2,1,0:T(8,128)S(1)}, f32[1,3,384,128]{3,2,1,0:T(8,128)}, u32[]{:S(2)}) copy-start(f32[1,3,384,128]{3,2,1,0:T(8,128)} %param.8) | copy-start | bytes 1769476
  17.9 10.8 %collective-permute-start.3 = (f32[3,96,128]{2,1,0:T(8,128)S(1)}, f32[3,96,128]{2,1,0:T(8,128)S(1)}, u32[]{:S(2)}, u32[]{:S(2)}) collective-permute-start(f32[3,96,128]{2,1,0:T(8,128)S(1)} %get-tuple-element.25), channel_id=1, source_target_pairs={{0,4},{1,5},{2,6},{3,7},{4,8},{5,9},{6,10},{7,11},{8,12},{9,13},{1... | collective-permute-start | bytes 442376 | tf_op jit(solution)/shard_map/ppermute | solution.py:126
  19.0 10.2 %collective-permute-start.4 = (f32[3,96,128]{2,1,0:T(8,128)S(1)}, f32[3,96,128]{2,1,0:T(8,128)S(1)}, u32[]{:S(2)}, u32[]{:S(2)}) collective-permute-start(f32[3,96,128]{2,1,0:T(8,128)S(1)} %get-tuple-element.26), channel_id=1, source_target_pairs={{0,5},{1,4},{2,7},{3,6},{4,9},{5,8},{6,11},{7,10},{8,13},{9,12},{1... | collective-permute-start | bytes 442376 | tf_op jit(solution)/shard_map/ppermute | solution.py:126
  19.0 15.1 %collective-permute-start.5 = (f32[3,96,128]{2,1,0:T(8,128)S(1)}, f32[3,96,128]{2,1,0:T(8,128)S(1)}, u32[]{:S(2)}, u32[]{:S(2)}) collective-permute-start(f32[3,96,128]{2,1,0:T(8,128)S(1)} %get-tuple-element.27), channel_id=1, source_target_pairs={{0,6},{1,7},{2,4},{3,5},{4,10},{5,11},{6,8},{7,9},{8,14},{9,15},{1... | collective-permute-start | bytes 442376 | tf_op jit(solution)/shard_map/ppermute | solution.py:126
  19.8 14.4 %collective-permute-start.6 = (f32[3,96,128]{2,1,0:T(8,128)S(1)}, f32[3,96,128]{2,1,0:T(8,128)S(1)}, u32[]{:S(2)}, u32[]{:S(2)}) collective-permute-start(f32[3,96,128]{2,1,0:T(8,128)S(1)} %get-tuple-element.28), channel_id=1, source_target_pairs={{0,7},{1,6},{2,5},{3,4},{4,11},{5,10},{6,9},{7,8},{8,15},{9,14},{1... | collective-permute-start | bytes 442376 | tf_op jit(solution)/shard_map/ppermute | solution.py:126
  23.2 10.9 %copy-start = (f32[1,3,96,512]{3,2,1,0:T(8,128)S(1)}, f32[1,3,96,512]{3,2,1,0:T(8,128)}, u32[]{:S(2)}) copy-start(f32[1,3,96,512]{3,2,1,0:T(8,128)} %param.6) | copy-start | bytes 1769476
  24.5 9.7 %collective-permute-start.8 = (f32[3,96,128]{2,1,0:T(8,128)S(1)}, f32[3,96,128]{2,1,0:T(8,128)S(1)}, u32[]{:S(2)}, u32[]{:S(2)}) collective-permute-start(f32[3,96,128]{2,1,0:T(8,128)S(1)} %get-tuple-element.34), channel_id=1, source_target_pairs={{0,1},{1,0},{2,3},{3,2},{4,5},{5,4},{6,7},{7,6},{8,9},{9,8},{10,11... | collective-permute-start | bytes 442376 | tf_op jit(solution)/shard_map/ppermute | solution.py:126
  28.7 10.0 %collective-permute-start.9 = (f32[3,96,128]{2,1,0:T(8,128)S(1)}, f32[3,96,128]{2,1,0:T(8,128)S(1)}, u32[]{:S(2)}, u32[]{:S(2)}) collective-permute-start(f32[3,96,128]{2,1,0:T(8,128)S(1)} %get-tuple-element.35), channel_id=1, source_target_pairs={{0,2},{1,3},{2,0},{3,1},{4,6},{5,7},{6,4},{7,5},{8,10},{9,11},{10,... | collective-permute-start | bytes 442376 | tf_op jit(solution)/shard_map/ppermute | solution.py:126
  29.2 10.0 %collective-permute-start.10 = (f32[3,96,128]{2,1,0:T(8,128)S(1)}, f32[3,96,128]{2,1,0:T(8,128)S(1)}, u32[]{:S(2)}, u32[]{:S(2)}) collective-permute-start(f32[3,96,128]{2,1,0:T(8,128)S(1)} %get-tuple-element.36), channel_id=1, source_target_pairs={{0,3},{1,2},{2,1},{3,0},{4,7},{5,6},{6,5},{7,4},{8,11},{9,10},{10,... | collective-permute-start | bytes 442376 | tf_op jit(solution)/shard_map/ppermute | solution.py:126

commit v3 on v2

v3 whole, which is shorter than its diff:
```python
import functools

import jax
import jax.numpy as jnp
from jax import lax
from jax.experimental import pallas as pl
from jax.experimental.pallas import tpu as pltpu
from jax.sharding import PartitionSpec as P

STEPS_MAX = 8
LANES = 128
HALF = LANES // 2


def split(values):
    high = values.astype(jnp.bfloat16)
    low = (values - high.astype(jnp.float32)).astype(jnp.bfloat16)
    return high, low


def swap_halves(values):
    return pltpu.roll(values, HALF, 1)


def left_half(shape):
    return lax.broadcasted_iota(jnp.int32, shape, 1) < HALF


def to_groups(first, second):
    left = left_half(first.shape)
    return jnp.where(left, first, swap_halves(second)), jnp.where(left, swap_halves(first), second)


def mirror_block(pieces, mirror_ref, block, rows, count):
    partner = count - 1 - block
    target = mirror_ref[block] - partner * rows
    lane = lax.broadcasted_iota(jnp.int32, (rows, rows), 0)
    one_hot = (lane == target).astype(jnp.bfloat16)
    values = jnp.concatenate(pieces, axis=1)
    high, low = split(values)
    return jnp.dot(
        jnp.concatenate([one_hot, one_hot], axis=1),
        jnp.concatenate([high, low], axis=0),
        preferred_element_type=jnp.float32,
    )


def prepare_kernel(count, rows, wall_ref, mirror_ref, end_ref, coupling_ref, ops_ref, ops_out, gains, base, *sends):
    wall = wall_ref[0]
    ny = ops_ref.shape[1]
    left = left_half((ny, LANES))
    for group in range(2):
        high, low = split(ops_ref[group])
        ops_out[group, :, 0:ny] = high
        ops_out[group, :, ny : 2 * ny] = high
        ops_out[group, :, 2 * ny : 3 * ny] = low
    gains[0, :, :LANES], gains[1, :, :LANES] = to_groups(coupling_ref[0], coupling_ref[1])
    gains[0, :, LANES:] = jnp.where(left, coupling_ref[2], 0.0)
    gains[1, :, LANES:] = jnp.where(left, 0.0, coupling_ref[2])
    base[0, :, :LANES], base[1, :, :LANES] = to_groups(end_ref[0], end_ref[1])
    base[0, :, LANES:] = end_ref[2]
    base[1, :, LANES:] = end_ref[2]
    for step in range(count):
        source = count - 1 - (wall ^ step)
        at = pl.ds(pl.multiple_of(source * rows, 8), rows)
        moved = mirror_block([end_ref[c, at, :] for c in range(3)], mirror_ref, source, rows, count)
        for c, sign in enumerate((1.0, -1.0, 1.0)):
            sends[step][c] = sign * moved[:, c * LANES : (c + 1) * LANES]


def adjoint_kernel(count, rows, wall_ref, steps_ref, mirror_ref, ops_ref, gains, base, *rest):
    pieces, outs = rest[:count], rest[count : 2 * count]
    scaled, state = rest[2 * count : 2 * count + 2], rest[2 * count + 2 :]
    wall = wall_ref[0]
    ny = base.shape[1]
    for step in range(count):
        block = wall ^ step
        partner = count - 1 - block
        at = pl.ds(pl.multiple_of(partner * rows, 8), rows)
        moved = mirror_block([pieces[step][c] for c in range(3)], mirror_ref, block, rows, count)
        pair = to_groups(moved[:, :LANES], -moved[:, LANES : 2 * LANES])
        for group in range(2):
            state[group][at, :LANES] = base[group, at, :LANES] - pair[group]
            state[group][at, LANES:] = base[group, at, LANES:] - moved[:, 2 * LANES :]

    def scale(group):
        high, low = split(gains[group] * state[group][...])
        scaled[group][0:ny] = high
        scaled[group][ny : 2 * ny] = low
        scaled[group][2 * ny : 3 * ny] = high

    def multiply(group):
        state[group][...] = jnp.dot(ops_ref[group], scaled[group][...], preferred_element_type=jnp.float32)

    def advance(_, carry):
        scale(1)
        multiply(0)
        scale(0)
        multiply(1)
        return carry

    def advance_some(_, carry):
        for _ in range(STEPS_MAX // 2):
            advance(0, 0)
        return carry

    steps = jnp.minimum(steps_ref[0], STEPS_MAX)
    scale(0)
    lax.fori_loop(0, steps // (STEPS_MAX // 2), advance_some, 0)
    lax.fori_loop(0, steps % (STEPS_MAX // 2), advance, 0)
    left = left_half((rows, LANES))
    for step in range(count):
        at = pl.ds(pl.multiple_of((wall ^ step) * rows, 8), rows)
        outs[step][0], outs[step][1] = to_groups(state[0][at, :LANES], state[1][at, :LANES])
        outs[step][2] = jnp.where(left, state[0][at, LANES:], state[1][at, LANES:])


def offset_kernel(count, wall_ref, start_ref, *rest):
    parts, out_ref = rest[:-1][::-1], rest[-1]
    wall = wall_ref[0]
    for step, part in enumerate(parts):
        at = pl.ds(pl.multiple_of((wall ^ step) * LANES, LANES), LANES)
        out_ref[:, :, at] = part[...] - start_ref[:, :, at]


def combine_kernel(count, wall_ref, offset_ref, *rest):
    parts, out_ref, held, sems = rest[:count][::-1], *rest[count:]
    wall = wall_ref[0]
    copies = []
    for c in range(3):
        for step, part in enumerate(parts):
            at = pl.ds(pl.multiple_of((wall ^ step) * LANES, LANES), LANES)
            held[c, :, at] = part[c] - offset_ref[c, :, at]
        copies.append(pltpu.make_async_copy(held.at[c], out_ref.at[c], sems.at[c]))
        copies[-1].start()
    for copy in copies:
        copy.wait()


def send(part, steps, flip, shape):
    slabs, count = shape
    pairs = [(t * count + w, (t + steps) % slabs * count + (w ^ flip)) for t in range(slabs) for w in range(count)]
    return lax.ppermute(part, ("tm", "wall"), pairs)


def on_device(shape, start_state, end_state, coupling, inverse_ops, mirror_rows, slab_steps):
    slabs, count = shape
    rows = start_state.shape[2]
    ny = end_state.shape[2]
    start, end, gain = start_state[0], end_state[0], coupling[0]
    wall = lax.axis_index("wall").astype(jnp.int32).reshape(1)
    mirror_blocks = mirror_rows.reshape(count, 1, rows)
    smem = pl.BlockSpec(memory_space=pltpu.SMEM)
    vmem = pl.BlockSpec(memory_space=pltpu.VMEM)
    part = jax.ShapeDtypeStruct((3, rows, LANES), jnp.float32)
    wide = jax.ShapeDtypeStruct((2, ny, 2 * LANES), jnp.float32)
    limit = pltpu.CompilerParams(vmem_limit_bytes=24 << 20)

    outgoing = [
        lax.dynamic_slice(start, (0, 0, (wall[0] ^ step) * LANES), (3, rows, LANES)) for step in range(count)
    ]
    incoming = [send(part, -1, step, shape) for step, part in enumerate(outgoing)]

    ops, gains, base, *mirrored = pl.pallas_call(
        functools.partial(prepare_kernel, count, rows),
        out_shape=[jax.ShapeDtypeStruct((2, ny, 3 * ny), jnp.bfloat16), wide, wide] + [part] * count,
        in_specs=[smem] + [vmem] * 4,
        out_specs=[vmem] * (3 + count),
        compiler_params=limit,
        cost_estimate=pl.CostEstimate(flops=10**8, bytes_accessed=4 << 20, transcendentals=0),
        name="prepare",
    )(wall, mirror_blocks, end, gain, inverse_ops)

    mirrored, arrived = lax.optimization_barrier((mirrored, incoming[:-1]))
    incoming = arrived + incoming[-1:]
    mirrored = [send(part, 1, i, shape) for i, part in enumerate(mirrored)]

    adjoint = pl.pallas_call(
        functools.partial(adjoint_kernel, count, rows),
        out_shape=[part] * count,
        in_specs=[smem, smem] + [vmem] * (4 + count),
        out_specs=[vmem] * count,
        scratch_shapes=[pltpu.VMEM((3 * ny, 2 * LANES), jnp.bfloat16)] * 2
        + [pltpu.VMEM((ny, 2 * LANES), jnp.float32)] * 2,
        compiler_params=limit,
        cost_estimate=pl.CostEstimate(flops=4 * 10**9, bytes_accessed=4 << 20, transcendentals=0),
        name="adjoint",
    )(wall, slab_steps, mirror_blocks, ops, gains, base, *incoming)
    returned = [adjoint[0]] + [send(adjoint[step], 0, step, shape) for step in range(1, count)]

    offset = pl.pallas_call(
        functools.partial(offset_kernel, count),
        out_shape=jax.ShapeDtypeStruct(start.shape, jnp.float32),
        in_specs=[smem, vmem] + [vmem] * count,
        out_specs=vmem,
        compiler_params=limit,
        cost_estimate=pl.CostEstimate(flops=10**6, bytes_accessed=40 << 20, transcendentals=0),
        name="offset",
    )(wall, start, *mirrored[::-1])
    gradient = pl.pallas_call(
        functools.partial(combine_kernel, count),
        out_shape=jax.ShapeDtypeStruct(start.shape, jnp.float32),
        in_specs=[smem, vmem] + [vmem] * count,
        out_specs=pl.BlockSpec(memory_space=pl.ANY),
        scratch_shapes=[pltpu.VMEM(start.shape, jnp.float32), pltpu.SemaphoreType.DMA((3,))],
        compiler_params=limit,
        cost_estimate=pl.CostEstimate(flops=10**6, bytes_accessed=3 << 20, transcendentals=0),
        name="combine",
    )(wall, offset, *returned[::-1])
    return gradient[None]


def solution(mesh):
    in_specs = (
        P("tm", None, "wall", None),
        P("tm", None, None, "wall"),
        P("tm", None, None, "wall"),
        P("wall", None, None),
        P(),
        P("tm"),
    )
    out_specs = P("tm", None, "wall", None)
    shape = (mesh.shape["tm"], mesh.shape["wall"])
    return jax.shard_map(
        functools.partial(on_device, shape),
        mesh=mesh,
        in_specs=in_specs,
        out_specs=out_specs,
        check_vma=False,
    )
```

time: 41.4 us -> 38.7 us (0.935); the launches traced: 40.6 us -> 38.7 us
  waiting for transfers between devices: 15.7 us -> 10.9 us
  Pallas kernels: 3.49 us -> 7.6 us
  starting transfers between devices: 17.6 us -> 15.3 us
  local copies, waits for them, and re-layouts: 3.1 us -> 4.16 us
    ppermute x11, waiting for transfers between devices: 15.7 us -> 10.9 us  [send(): return lax.ppermute(part, ('tm', 'wall'), pairs)]
    pallas_call x1, Pallas kernels: 1.33 us -> 5.9 us  [on_device(): pl.pallas_call(functools.partial(adjoint_kernel, count, rows), out_shape=...]
    ppermute x11, starting transfers between devices: 17.6 us -> 15.3 us  [send(): return lax.ppermute(part, ('tm', 'wall'), pairs)]
    unnamed x8, local copies, waits for them, and re-layouts: 1.07 us -> 2.13 us
    pallas_call x1, Pallas kernels: 1.46 us -> 0.87 us  [on_device(): pl.pallas_call(functools.partial(combine_kernel, count), out_shape=jax.Sh...]
  transfers between devices with their start and end apart: 11 -> 11, of which waited for: 6 -> 6; matrix products, arithmetic and copies ran while one was open for 2% -> 2% of each run, Pallas kernels for 5% -> 17%
where the time goes in v3:
time: 38.7 us
  starting transfers between devices  15.3 us (40%)
  waiting for transfers between devices  10.9 us (28%)
  Pallas kernels  7.6 us (20%)
  local copies, waits for them, and re-layouts  4.16 us (11%)
  between operations  0.74 us (2%)
    ppermute x11, starting transfers between devices, send(): return lax.ppermute(part, ('tm', 'wall'), pairs)  15.3 us
    ppermute x11, waiting for transfers between devices, send(): return lax.ppermute(part, ('tm', 'wall'), pairs)  10.9 us
    pallas_call x1, Pallas kernels, on_device(): pl.pallas_call(functools.partial(adjoint_kernel, count, rows), out_shape=...  5.9 us
    unnamed x8, local copies, waits for them, and re-layouts  2.13 us
    dynamic_slice x1, local copies, waits for them, and re-layouts, on_device(): lax.dynamic_slice(start, (0, 0, (wall[0] ^ step) * LANES), (3, rows, LANES))  1.27 us
    pallas_call x1, Pallas kernels, on_device(): pl.pallas_call(functools.partial(combine_kernel, count), out_shape=jax.Sh...  0.87 us
  transfers between devices with their start and end apart: 11, of which 6 were waited for; matrix products, arithmetic and copies ran while one was open for 2% of the time, Pallas kernels for 17%

profile of v3, /device:TPU:0, one launch (start us, length us, event | category | flops | bytes accessed | tf_op | source)
XLA Modules:
  0.0 38.7 jit_solution(16513209687454105652)
XLA Ops:
  0.0 0.0 copy-start.1
  0.0 1.3 %dynamic-slice_bitcast_fusion = (f32[3,96,128]{2,1,0:T(8,128)S(1)}, f32[3,96,128]{2,1,0:T(8,128)S(1)}, f32[3,96,128]{2,1,0:T(8,128)S(1)}, f32[3,96,128]{2,1,0:T(8,128)S(1)}) fusion(f32[1,3,96,512]{3,2,1,0:T(8,128)} %param.6, s32[]{:T(128)S(6)} %select_n.15, s32[]{:T(128)S(6)} %select_n.13, s32[]{:T(128)S(6)} %select_n.12, s32[]{:T(128)S(6)} %select_n.14), kind=kLoop, calls=%fused_computation | loop fusion | bytes 1179664 | tf_op jit(solution)/shard_map/dynamic_slice | solution.py:160
  1.3 6.0 %collective-permute-start = (f32[3,96,128]{2,1,0:T(8,128)S(1)}, f32[3,96,128]{2,1,0:T(8,128)S(1)}, u32[]{:S(2)}, u32[]{:S(2)}) collective-permute-start(f32[3,96,128]{2,1,0:T(8,128)S(1)} %get-tuple-element.43), channel_id=1, source_target_pairs={{0,28},{1,29},{2,30},{3,31},{4,0},{5,1},{6,2},{7,3},{8,4},{9,5},{1... | collective-permute-start | bytes 442376 | tf_op jit(solution)/shard_map/ppermute | solution.py:143
  7.3 0.0 collective-permute-start.1
  7.3 2.0 %collective-permute-start.2 = (f32[3,96,128]{2,1,0:T(8,128)S(1)}, f32[3,96,128]{2,1,0:T(8,128)S(1)}, u32[]{:S(2)}, u32[]{:S(2)}) collective-permute-start(f32[3,96,128]{2,1,0:T(8,128)S(1)} %get-tuple-element.44), channel_id=1, source_target_pairs={{0,30},{1,31},{2,28},{3,29},{4,2},{5,3},{6,0},{7,1},{8,6},{9,7},{1... | collective-permute-start | bytes 442376 | tf_op jit(solution)/shard_map/ppermute | solution.py:143
  9.3 0.8 %collective-permute-start.7 = (f32[3,96,128]{2,1,0:T(8,128)S(1)}, f32[3,96,128]{2,1,0:T(8,128)S(1)}, u32[]{:S(2)}, u32[]{:S(2)}) collective-permute-start(f32[3,96,128]{2,1,0:T(8,128)S(1)} %get-tuple-element.41), channel_id=1, source_target_pairs={{0,31},{1,30},{2,29},{3,28},{4,3},{5,2},{6,1},{7,0},{8,7},{9,6},{1... | collective-permute-start | bytes 442376 | tf_op jit(solution)/shard_map/ppermute | solution.py:143
  10.1 0.8 %reshape.11.mirror_ref = s32[4,1,96]{2,1,0:T(1,128)S(1)} reshape(s32[384]{0:T(512)} %param.10) | data formatting | bytes 3072 | tf_op jit(solution)/shard_map/reshape | solution.py:152
  11.5 0.0 copy-done.1
  11.5 0.0 copy-start.2
  11.5 1.1 %copy-done.2 = f32[1,3,384,128]{3,2,1,0:T(8,128)S(1)} copy-done((f32[1,3,384,128]{3,2,1,0:T(8,128)S(1)}, f32[1,3,384,128]{3,2,1,0:T(8,128)}, u32[]{:S(2)}) %copy-start.2) | copy-done | bytes 589848
  12.6 0.0 copy-start.3
  12.6 1.1 %copy-done.3 = f32[1,3,384,128]{3,2,1,0:T(8,128)S(1)} copy-done((f32[1,3,384,128]{3,2,1,0:T(8,128)S(1)}, f32[1,3,384,128]{3,2,1,0:T(8,128)}, u32[]{:S(2)}) %copy-start.3) | copy-done | bytes 589848
  13.6 0.7 %prepare.1 = (bf16[2,384,1152]{2,1,0:T(8,128)(2,1)S(1)}, f32[2,384,256]{2,1,0:T(8,128)S(1)}, f32[2,384,256]{2,1,0:T(8,128)S(1)}, f32[3,96,128]{2,1,0:T(8,128)S(1...) custom-call(s32[1]{0:T(128)} %bitcast.wall_ref, ...), custom_call_target="tpu_custom_call" | custom-call | flops 100000000 | bytes 4194304 | tf_op jit(solution)/shard_map/prepare/pallas_call | solution.py:164
  14.4 0.0 collective-permute-done.rest_0_
  14.4 0.3 collective-permute-done.1.rest_1_
  14.7 3.2 %collective-permute-done.2.rest_2_ = f32[3,96,128]{2,1,0:T(8,128)S(1)} collective-permute-done((f32[3,96,128]{2,1,0:T(8,128)S(1)}, f32[3,96,128]{2,1,0:T(8,128)S(1)}, u32[]{:S(2)}, u32[]{:S(2)}) %collective-permute-start.2) | collective-permute-done | bytes 147488 | tf_op jit(solution)/shard_map/ppermute | solution.py:143
  17.9 0.0 collective-permute-start.3
  17.9 0.3 collective-permute-start.4
  18.2 4.4 %collective-permute-start.5 = (f32[3,96,128]{2,1,0:T(8,128)S(1)}, f32[3,96,128]{2,1,0:T(8,128)S(1)}, u32[]{:S(2)}, u32[]{:S(2)}) collective-permute-start(f32[3,96,128]{2,1,0:T(8,128)S(1)} %get-tuple-element.29), channel_id=1, source_target_pairs={{0,5},{1,4},{2,7},{3,6},{4,9},{5,8},{6,11},{7,10},{8,13},{9,12},{1... | collective-permute-start | bytes 442376 | tf_op jit(solution)/shard_map/ppermute | solution.py:143
  22.6 0.6 %collective-permute-start.6 = (f32[3,96,128]{2,1,0:T(8,128)S(1)}, f32[3,96,128]{2,1,0:T(8,128)S(1)}, u32[]{:S(2)}, u32[]{:S(2)}) collective-permute-start(f32[3,96,128]{2,1,0:T(8,128)S(1)} %get-tuple-element.30), channel_id=1, source_target_pairs={{0,4},{1,5},{2,6},{3,7},{4,8},{5,9},{6,10},{7,11},{8,12},{9,13},{1... | collective-permute-start | bytes 442376 | tf_op jit(solution)/shard_map/ppermute | solution.py:143
  23.2 0.0 collective-permute-done.7.rest_3_
  23.2 0.0 copy-start
  23.2 5.9 %adjoint.1 = (f32[3,96,128]{2,1,0:T(8,128)S(1)}, f32[3,96,128]{2,1,0:T(8,128)S(1)}, f32[3,96,128]{2,1,0:T(8,128)S(1)}, f32[3,96,128]{2,1,0:T(8,128)S(1)}) custom-call(s32[1]{0:T(128)} %bitcast.wall_ref, s32[1]{0:T(128)S(6)} %copy.7.steps_ref, s32[4,1,96]{2,1,0:T(1,128)S(1)} %reshape.11.mirror_ref, bf16[2,384,1152]{2,1,0:T(8,128)(2,1)S(1)} %get-tuple-element.31.ops_ref, ...), custom_call_target="tpu_custom_call" | custom-call | flops 4000000000 | bytes 4194304 | tf_op jit(solution)/shard_map/adjoint/pallas_call | solution.py:178
  29.1 0.1 collective-permute-start.8
  29.2 0.0 collective-permute-done.3.rest_0_
  29.2 1.1 %collective-permute-start.9 = (f32[3,96,128]{2,1,0:T(8,128)S(1)}, f32[3,96,128]{2,1,0:T(8,128)S(1)}, u32[]{:S(2)}, u32[]{:S(2)}) collective-permute-start(f32[3,96,128]{2,1,0:T(8,128)S(1)} %get-tuple-element.38), channel_id=1, source_target_pairs={{0,2},{1,3},{2,0},{3,1},{4,6},{5,7},{6,4},{7,5},{8,10},{9,11},{10,... | collective-permute-start | bytes 442376 | tf_op jit(solution)/shard_map/ppermute | solution.py:143
  30.3 1.5 %collective-permute-done.4.rest_1_ = f32[3,96,128]{2,1,0:T(8,128)S(1)} collective-permute-done((f32[3,96,128]{2,1,0:T(8,128)S(1)}, f32[3,96,128]{2,1,0:T(8,128)S(1)}, u32[]{:S(2)}, u32[]{:S(2)}) %collective-permute-start.4) | collective-permute-done | bytes 147488 | tf_op jit(solution)/shard_map/ppermute | solution.py:143
  31.8 0.0 collective-permute-start.10
  31.8 1.1 %collective-permute-done.5.rest_2_ = f32[3,96,128]{2,1,0:T(8,128)S(1)} collective-permute-done((f32[3,96,128]{2,1,0:T(8,128)S(1)}, f32[3,96,128]{2,1,0:T(8,128)S(1)}, u32[]{:S(2)}, u32[]{:S(2)}) %collective-permute-start.5) | collective-permute-done | bytes 147488 | tf_op jit(solution)/shard_map/ppermute | solution.py:143
  33.0 4.2 %collective-permute-done.6.rest_3_ = f32[3,96,128]{2,1,0:T(8,128)S(1)} collective-permute-done((f32[3,96,128]{2,1,0:T(8,128)S(1)}, f32[3,96,128]{2,1,0:T(8,128)S(1)}, u32[]{:S(2)}, u32[]{:S(2)}) %collective-permute-start.6) | collective-permute-done | bytes 147488 | tf_op jit(solution)/shard_map/ppermute | solution.py:143
  37.2 0.0 copy-done
  37.2 0.1 offset.1.offset_ref
  37.3 0.0 collective-permute-done.8.rest_0_
  37.3 0.6 %collective-permute-done.9.rest_1_ = f32[3,96,128]{2,1,0:T(8,128)S(1)} collective-permute-done((f32[3,96,128]{2,1,0:T(8,128)S(1)}, f32[3,96,128]{2,1,0:T(8,128)S(1)}, u32[]{:S(2)}, u32[]{:S(2)}) %collective-permute-start.9) | collective-permute-done | bytes 147488 | tf_op jit(solution)/shard_map/ppermute | solution.py:143
  37.8 0.0 collective-permute-done.10.rest_2_
  37.8 0.9 %combine.1 = f32[3,96,512]{2,1,0:T(8,128)} custom-call(s32[1]{0:T(128)} %bitcast.wall_ref, f32[3,96,512]{2,1,0:T(8,128)S(1)} %offset.1.offset_ref, f32[3,96,128]{2,1,0:T(8,128)S(1)} %collective-permute-done.8.rest_0_, f32[3,96,128]{2,1,0:T(8,128)S(1)} %collective-permute-done.9.rest_1_, f32[3,96,128]{2,1,0:T(8,128)S(1)} %collective-permute-done.10.rest_2_, ...), custom_call_target="tpu_custom_call" | custom-call | flops 1000000 | bytes 3145728 | tf_op jit(solution)/shard_map/combine/pallas_call | solution.py:200
Async XLA Ops:
  0.0 11.5 %copy-start.1 = (f32[2,384,384]{2,1,0:T(8,128)S(1)}, f32[2,384,384]{2,1,0:T(8,128)}, u32[]{:S(2)}) copy-start(f32[2,384,384]{2,1,0:T(8,128)} %ops_ref.1) | copy-start | bytes 3538948
  1.3 13.1 %collective-permute-start = (f32[3,96,128]{2,1,0:T(8,128)S(1)}, f32[3,96,128]{2,1,0:T(8,128)S(1)}, u32[]{:S(2)}, u32[]{:S(2)}) collective-permute-start(f32[3,96,128]{2,1,0:T(8,128)S(1)} %get-tuple-element.43), channel_id=1, source_target_pairs={{0,28},{1,29},{2,30},{3,31},{4,0},{5,1},{6,2},{7,3},{8,4},{9,5},{1... | collective-permute-start | bytes 442376 | tf_op jit(solution)/shard_map/ppermute | solution.py:143
  7.3 7.4 %collective-permute-start.1 = (f32[3,96,128]{2,1,0:T(8,128)S(1)}, f32[3,96,128]{2,1,0:T(8,128)S(1)}, u32[]{:S(2)}, u32[]{:S(2)}) collective-permute-start(f32[3,96,128]{2,1,0:T(8,128)S(1)} %get-tuple-element.42), channel_id=1, source_target_pairs={{0,29},{1,28},{2,31},{3,30},{4,1},{5,0},{6,3},{7,2},{8,5},{9,4},{1... | collective-permute-start | bytes 442376 | tf_op jit(solution)/shard_map/ppermute | solution.py:143
  7.3 10.6 %collective-permute-start.2 = (f32[3,96,128]{2,1,0:T(8,128)S(1)}, f32[3,96,128]{2,1,0:T(8,128)S(1)}, u32[]{:S(2)}, u32[]{:S(2)}) collective-permute-start(f32[3,96,128]{2,1,0:T(8,128)S(1)} %get-tuple-element.44), channel_id=1, source_target_pairs={{0,30},{1,31},{2,28},{3,29},{4,2},{5,3},{6,0},{7,1},{8,6},{9,7},{1... | collective-permute-start | bytes 442376 | tf_op jit(solution)/shard_map/ppermute | solution.py:143
  9.3 13.9 %collective-permute-start.7 = (f32[3,96,128]{2,1,0:T(8,128)S(1)}, f32[3,96,128]{2,1,0:T(8,128)S(1)}, u32[]{:S(2)}, u32[]{:S(2)}) collective-permute-start(f32[3,96,128]{2,1,0:T(8,128)S(1)} %get-tuple-element.41), channel_id=1, source_target_pairs={{0,31},{1,30},{2,29},{3,28},{4,3},{5,2},{6,1},{7,0},{8,7},{9,6},{1... | collective-permute-start | bytes 442376 | tf_op jit(solution)/shard_map/ppermute | solution.py:143
  11.5 1.1 %copy-start.2 = (f32[1,3,384,128]{3,2,1,0:T(8,128)S(1)}, f32[1,3,384,128]{3,2,1,0:T(8,128)}, u32[]{:S(2)}) copy-start(f32[1,3,384,128]{3,2,1,0:T(8,128)} %param.7) | copy-start | bytes 1769476
  12.6 1.1 %copy-start.3 = (f32[1,3,384,128]{3,2,1,0:T(8,128)S(1)}, f32[1,3,384,128]{3,2,1,0:T(8,128)}, u32[]{:S(2)}) copy-start(f32[1,3,384,128]{3,2,1,0:T(8,128)} %param.8) | copy-start | bytes 1769476
  17.9 11.3 %collective-permute-start.3 = (f32[3,96,128]{2,1,0:T(8,128)S(1)}, f32[3,96,128]{2,1,0:T(8,128)S(1)}, u32[]{:S(2)}, u32[]{:S(2)}) collective-permute-start(f32[3,96,128]{2,1,0:T(8,128)S(1)} %get-tuple-element.27), channel_id=1, source_target_pairs={{0,7},{1,6},{2,5},{3,4},{4,11},{5,10},{6,9},{7,8},{8,15},{9,14},{1... | collective-permute-start | bytes 442376 | tf_op jit(solution)/shard_map/ppermute | solution.py:143
  17.9 13.9 %collective-permute-start.4 = (f32[3,96,128]{2,1,0:T(8,128)S(1)}, f32[3,96,128]{2,1,0:T(8,128)S(1)}, u32[]{:S(2)}, u32[]{:S(2)}) collective-permute-start(f32[3,96,128]{2,1,0:T(8,128)S(1)} %get-tuple-element.28), channel_id=1, source_target_pairs={{0,6},{1,7},{2,4},{3,5},{4,10},{5,11},{6,8},{7,9},{8,14},{9,15},{1... | collective-permute-start | bytes 442376 | tf_op jit(solution)/shard_map/ppermute | solution.py:143
  18.2 14.8 %collective-permute-start.5 = (f32[3,96,128]{2,1,0:T(8,128)S(1)}, f32[3,96,128]{2,1,0:T(8,128)S(1)}, u32[]{:S(2)}, u32[]{:S(2)}) collective-permute-start(f32[3,96,128]{2,1,0:T(8,128)S(1)} %get-tuple-element.29), channel_id=1, source_target_pairs={{0,5},{1,4},{2,7},{3,6},{4,9},{5,8},{6,11},{7,10},{8,13},{9,12},{1... | collective-permute-start | bytes 442376 | tf_op jit(solution)/shard_map/ppermute | solution.py:143
  22.6 14.6 %collective-permute-start.6 = (f32[3,96,128]{2,1,0:T(8,128)S(1)}, f32[3,96,128]{2,1,0:T(8,128)S(1)}, u32[]{:S(2)}, u32[]{:S(2)}) collective-permute-start(f32[3,96,128]{2,1,0:T(8,128)S(1)} %get-tuple-element.30), channel_id=1, source_target_pairs={{0,4},{1,5},{2,6},{3,7},{4,8},{5,9},{6,10},{7,11},{8,12},{9,13},{1... | collective-permute-start | bytes 442376 | tf_op jit(solution)/shard_map/ppermute | solution.py:143
  23.2 14.0 %copy-start = (f32[1,3,96,512]{3,2,1,0:T(8,128)S(1)}, f32[1,3,96,512]{3,2,1,0:T(8,128)}, u32[]{:S(2)}) copy-start(f32[1,3,96,512]{3,2,1,0:T(8,128)} %param.6) | copy-start | bytes 1769476
  29.1 8.2 %collective-permute-start.8 = (f32[3,96,128]{2,1,0:T(8,128)S(1)}, f32[3,96,128]{2,1,0:T(8,128)S(1)}, u32[]{:S(2)}, u32[]{:S(2)}) collective-permute-start(f32[3,96,128]{2,1,0:T(8,128)S(1)} %get-tuple-element.37), channel_id=1, source_target_pairs={{0,3},{1,2},{2,1},{3,0},{4,7},{5,6},{6,5},{7,4},{8,11},{9,10},{10,... | collective-permute-start | bytes 442376 | tf_op jit(solution)/shard_map/ppermute | solution.py:143
  29.2 8.6 %collective-permute-start.9 = (f32[3,96,128]{2,1,0:T(8,128)S(1)}, f32[3,96,128]{2,1,0:T(8,128)S(1)}, u32[]{:S(2)}, u32[]{:S(2)}) collective-permute-start(f32[3,96,128]{2,1,0:T(8,128)S(1)} %get-tuple-element.38), channel_id=1, source_target_pairs={{0,2},{1,3},{2,0},{3,1},{4,6},{5,7},{6,4},{7,5},{8,10},{9,11},{10,... | collective-permute-start | bytes 442376 | tf_op jit(solution)/shard_map/ppermute | solution.py:143
  31.8 6.0 %collective-permute-start.10 = (f32[3,96,128]{2,1,0:T(8,128)S(1)}, f32[3,96,128]{2,1,0:T(8,128)S(1)}, u32[]{:S(2)}, u32[]{:S(2)}) collective-permute-start(f32[3,96,128]{2,1,0:T(8,128)S(1)} %get-tuple-element.39), channel_id=1, source_target_pairs={{0,1},{1,0},{2,3},{3,2},{4,5},{5,4},{6,7},{7,6},{8,9},{9,8},{10,11... | collective-permute-start | bytes 442376 | tf_op jit(solution)/shard_map/ppermute | solution.py:143

commit v4 on v3

--- a/solution.py
+++ b/solution.py
@@ -161,6 +161,7 @@
     ]
     incoming = [send(part, -1, step, shape) for step, part in enumerate(outgoing)]
 
+    end, incoming[:2] = lax.optimization_barrier((end, incoming[:2]))
     ops, gains, base, *mirrored = pl.pallas_call(
         functools.partial(prepare_kernel, count, rows),
         out_shape=[jax.ShapeDtypeStruct((2, ny, 3 * ny), jnp.bfloat16), wide, wide] + [part] * count,
@@ -171,8 +172,6 @@
         name="prepare",
     )(wall, mirror_blocks, end, gain, inverse_ops)
 
-    mirrored, arrived = lax.optimization_barrier((mirrored, incoming[:-1]))
-    incoming = arrived + incoming[-1:]
     mirrored = [send(part, 1, i, shape) for i, part in enumerate(mirrored)]
 
     adjoint = pl.pallas_call(

time: 38.7 us -> 37 us (0.956)
  Pallas kernels: 7.6 us -> 3.11 us
  starting transfers between devices: 15.3 us -> 17.1 us
  waiting for transfers between devices: 10.9 us -> 11.6 us
    pallas_call x1, Pallas kernels: 5.9 us -> 1.41 us  [on_device(): pl.pallas_call(functools.partial(adjoint_kernel, count, rows), out_shape=...]
    ppermute x11, starting transfers between devices: 15.3 us -> 17.1 us  [send(): return lax.ppermute(part, ('tm', 'wall'), pairs)]
    ppermute x11, waiting for transfers between devices: 10.9 us -> 11.6 us  [send(): return lax.ppermute(part, ('tm', 'wall'), pairs)]
  transfers between devices with their start and end apart: 11 -> 11, of which waited for: 6 -> 6; matrix products, arithmetic and copies ran while one was open for 2% -> 2% of each run, Pallas kernels for 17% -> 6%
where the time goes in v4:
time: 37 us; the launch traced here: 36.7 us
  starting transfers between devices  17.1 us (46%)
  waiting for transfers between devices  11.6 us (31%)
  local copies, waits for them, and re-layouts  4.17 us (11%)
  Pallas kernels  3.11 us (8%)
  between operations  0.7 us (2%)
    ppermute x11, starting transfers between devices, send(): return lax.ppermute(part, ('tm', 'wall'), pairs)  17.1 us
    ppermute x11, waiting for transfers between devices, send(): return lax.ppermute(part, ('tm', 'wall'), pairs)  11.6 us
    unnamed x8, local copies, waits for them, and re-layouts  2.14 us
    pallas_call x1, Pallas kernels, on_device(): pl.pallas_call(functools.partial(adjoint_kernel, count, rows), out_shape=...  1.41 us
    dynamic_slice x1, local copies, waits for them, and re-layouts, on_device(): lax.dynamic_slice(start, (0, 0, (wall[0] ^ step) * LANES), (3, rows, LANES))  1.27 us
    pallas_call x1, Pallas kernels, on_device(): pl.pallas_call(functools.partial(combine_kernel, count), out_shape=jax.Sh...  0.87 us
    reshape x1, local copies, waits for them, and re-layouts, on_device(): mirror_blocks = mirror_rows.reshape(count, 1, rows)  0.76 us
  transfers between devices with their start and end apart: 11, of which 6 were waited for; matrix products, arithmetic and copies ran while one was open for 2% of the time, Pallas kernels for 6%

profile of v4, /device:TPU:0, one launch (start us, length us, event | category | flops | bytes accessed | tf_op | source)
XLA Modules:
  0.0 36.7 jit_solution(14414305775229492469)
XLA Ops:
  0.0 0.0 copy-start.1
  0.0 1.3 %dynamic-slice_bitcast_fusion = (f32[3,96,128]{2,1,0:T(8,128)S(1)}, f32[3,96,128]{2,1,0:T(8,128)S(1)}, f32[3,96,128]{2,1,0:T(8,128)S(1)}, f32[3,96,128]{2,1,0:T(8,128)S(1)}) fusion(f32[1,3,96,512]{3,2,1,0:T(8,128)} %param.6, s32[]{:T(128)S(6)} %select_n.15, s32[]{:T(128)S(6)} %select_n.13, s32[]{:T(128)S(6)} %select_n.12, s32[]{:T(128)S(6)} %select_n.14), kind=kLoop, calls=%fused_computation | loop fusion | bytes 1179664 | tf_op jit(solution)/shard_map/dynamic_slice | solution.py:160
  1.3 6.0 %collective-permute-start = (f32[3,96,128]{2,1,0:T(8,128)S(1)}, f32[3,96,128]{2,1,0:T(8,128)S(1)}, u32[]{:S(2)}, u32[]{:S(2)}) collective-permute-start(f32[3,96,128]{2,1,0:T(8,128)S(1)} %get-tuple-element.35), channel_id=1, source_target_pairs={{0,28},{1,29},{2,30},{3,31},{4,0},{5,1},{6,2},{7,3},{8,4},{9,5},{1... | collective-permute-start | bytes 442376 | tf_op jit(solution)/shard_map/ppermute | solution.py:143
  7.3 0.0 collective-permute-start.1
  7.3 2.0 %collective-permute-start.6 = (f32[3,96,128]{2,1,0:T(8,128)S(1)}, f32[3,96,128]{2,1,0:T(8,128)S(1)}, u32[]{:S(2)}, u32[]{:S(2)}) collective-permute-start(f32[3,96,128]{2,1,0:T(8,128)S(1)} %get-tuple-element.36), channel_id=1, source_target_pairs={{0,30},{1,31},{2,28},{3,29},{4,2},{5,3},{6,0},{7,1},{8,6},{9,7},{1... | collective-permute-start | bytes 442376 | tf_op jit(solution)/shard_map/ppermute | solution.py:143
  9.3 0.8 %collective-permute-start.7 = (f32[3,96,128]{2,1,0:T(8,128)S(1)}, f32[3,96,128]{2,1,0:T(8,128)S(1)}, u32[]{:S(2)}, u32[]{:S(2)}) collective-permute-start(f32[3,96,128]{2,1,0:T(8,128)S(1)} %get-tuple-element.33), channel_id=1, source_target_pairs={{0,31},{1,30},{2,29},{3,28},{4,3},{5,2},{6,1},{7,0},{8,7},{9,6},{1... | collective-permute-start | bytes 442376 | tf_op jit(solution)/shard_map/ppermute | solution.py:143
  10.1 0.8 %reshape.11.mirror_ref = s32[4,1,96]{2,1,0:T(1,128)S(1)} reshape(s32[384]{0:T(512)} %param.10) | data formatting | bytes 3072 | tf_op jit(solution)/shard_map/reshape | solution.py:152
  11.5 0.1 collective-permute-done.rest_0_
  11.6 3.2 %collective-permute-done.1.rest_1_ = f32[3,96,128]{2,1,0:T(8,128)S(1)} collective-permute-done((f32[3,96,128]{2,1,0:T(8,128)S(1)}, f32[3,96,128]{2,1,0:T(8,128)S(1)}, u32[]{:S(2)}, u32[]{:S(2)}) %collective-permute-start.1) | collective-permute-done | bytes 147488 | tf_op jit(solution)/shard_map/ppermute | solution.py:143
  14.7 0.0 copy-done.1
  14.7 0.0 copy-start.2
  14.7 1.1 %copy-done.2 = f32[1,3,384,128]{3,2,1,0:T(8,128)S(1)} copy-done((f32[1,3,384,128]{3,2,1,0:T(8,128)S(1)}, f32[1,3,384,128]{3,2,1,0:T(8,128)}, u32[]{:S(2)}) %copy-start.2) | copy-done | bytes 589848
  15.8 0.0 copy-start.3
  15.8 1.1 %copy-done.3 = f32[1,3,384,128]{3,2,1,0:T(8,128)S(1)} copy-done((f32[1,3,384,128]{3,2,1,0:T(8,128)S(1)}, f32[1,3,384,128]{3,2,1,0:T(8,128)}, u32[]{:S(2)}) %copy-start.3) | copy-done | bytes 589848
  16.8 0.7 %prepare.1 = (bf16[2,384,1152]{2,1,0:T(8,128)(2,1)S(1)}, f32[2,384,256]{2,1,0:T(8,128)S(1)}, f32[2,384,256]{2,1,0:T(8,128)S(1)}, f32[3,96,128]{2,1,0:T(8,128)S(1...) custom-call(s32[1]{0:T(128)} %bitcast.wall_ref, ...), custom_call_target="tpu_custom_call" | custom-call | flops 100000000 | bytes 4194304 | tf_op jit(solution)/shard_map/prepare/pallas_call | solution.py:165
  17.6 0.9 %collective-permute-start.2 = (f32[3,96,128]{2,1,0:T(8,128)S(1)}, f32[3,96,128]{2,1,0:T(8,128)S(1)}, u32[]{:S(2)}, u32[]{:S(2)}) collective-permute-start(f32[3,96,128]{2,1,0:T(8,128)S(1)} %get-tuple-element.20), channel_id=1, source_target_pairs={{0,7},{1,6},{2,5},{3,4},{4,11},{5,10},{6,9},{7,8},{8,15},{9,14},{1... | collective-permute-start | bytes 442376 | tf_op jit(solution)/shard_map/ppermute | solution.py:143
  18.5 0.5 %collective-permute-start.3 = (f32[3,96,128]{2,1,0:T(8,128)S(1)}, f32[3,96,128]{2,1,0:T(8,128)S(1)}, u32[]{:S(2)}, u32[]{:S(2)}) collective-permute-start(f32[3,96,128]{2,1,0:T(8,128)S(1)} %get-tuple-element.21), channel_id=1, source_target_pairs={{0,6},{1,7},{2,4},{3,5},{4,10},{5,11},{6,8},{7,9},{8,14},{9,15},{1... | collective-permute-start | bytes 442376 | tf_op jit(solution)/shard_map/ppermute | solution.py:143
  19.0 0.4 %collective-permute-start.4 = (f32[3,96,128]{2,1,0:T(8,128)S(1)}, f32[3,96,128]{2,1,0:T(8,128)S(1)}, u32[]{:S(2)}, u32[]{:S(2)}) collective-permute-start(f32[3,96,128]{2,1,0:T(8,128)S(1)} %get-tuple-element.22), channel_id=1, source_target_pairs={{0,5},{1,4},{2,7},{3,6},{4,9},{5,8},{6,11},{7,10},{8,13},{9,12},{1... | collective-permute-start | bytes 442376 | tf_op jit(solution)/shard_map/ppermute | solution.py:143
  19.3 0.0 collective-permute-done.6.rest_2_
  19.3 2.2 %collective-permute-start.5 = (f32[3,96,128]{2,1,0:T(8,128)S(1)}, f32[3,96,128]{2,1,0:T(8,128)S(1)}, u32[]{:S(2)}, u32[]{:S(2)}) collective-permute-start(f32[3,96,128]{2,1,0:T(8,128)S(1)} %get-tuple-element.23), channel_id=1, source_target_pairs={{0,4},{1,5},{2,6},{3,7},{4,8},{5,9},{6,10},{7,11},{8,12},{9,13},{1... | collective-permute-start | bytes 442376 | tf_op jit(solution)/shard_map/ppermute | solution.py:143
  21.5 0.0 collective-permute-done.7.rest_3_
  21.5 0.0 copy-start
  21.5 1.4 %adjoint.1 = (f32[3,96,128]{2,1,0:T(8,128)S(1)}, f32[3,96,128]{2,1,0:T(8,128)S(1)}, f32[3,96,128]{2,1,0:T(8,128)S(1)}, f32[3,96,128]{2,1,0:T(8,128)S(1)}) custom-call(s32[1]{0:T(128)} %bitcast.wall_ref, s32[1]{0:T(128)S(6)} %copy.7.steps_ref, s32[4,1,96]{2,1,0:T(1,128)S(1)} %reshape.11.mirror_ref, bf16[2,384,1152]{2,1,0:T(8,128)(2,1)S(1)} %get-tuple-element.24.ops_ref, ...), custom_call_target="tpu_custom_call" | custom-call | flops 4000000000 | bytes 4194304 | tf_op jit(solution)/shard_map/adjoint/pallas_call | solution.py:177
  22.9 1.8 %collective-permute-start.8 = (f32[3,96,128]{2,1,0:T(8,128)S(1)}, f32[3,96,128]{2,1,0:T(8,128)S(1)}, u32[]{:S(2)}, u32[]{:S(2)}) collective-permute-start(f32[3,96,128]{2,1,0:T(8,128)S(1)} %get-tuple-element.29), channel_id=1, source_target_pairs={{0,3},{1,2},{2,1},{3,0},{4,7},{5,6},{6,5},{7,4},{8,11},{9,10},{10,... | collective-permute-start | bytes 442376 | tf_op jit(solution)/shard_map/ppermute | solution.py:143
  24.7 2.4 %collective-permute-done.2.rest_0_ = f32[3,96,128]{2,1,0:T(8,128)S(1)} collective-permute-done((f32[3,96,128]{2,1,0:T(8,128)S(1)}, f32[3,96,128]{2,1,0:T(8,128)S(1)}, u32[]{:S(2)}, u32[]{:S(2)}) %collective-permute-start.2) | collective-permute-done | bytes 147488 | tf_op jit(solution)/shard_map/ppermute | solution.py:143
  27.1 1.4 %collective-permute-start.9 = (f32[3,96,128]{2,1,0:T(8,128)S(1)}, f32[3,96,128]{2,1,0:T(8,128)S(1)}, u32[]{:S(2)}, u32[]{:S(2)}) collective-permute-start(f32[3,96,128]{2,1,0:T(8,128)S(1)} %get-tuple-element.30), channel_id=1, source_target_pairs={{0,2},{1,3},{2,0},{3,1},{4,6},{5,7},{6,4},{7,5},{8,10},{9,11},{10,... | collective-permute-start | bytes 442376 | tf_op jit(solution)/shard_map/ppermute | solution.py:143
  28.5 0.3 collective-permute-done.3.rest_1_
  28.9 1.2 %collective-permute-start.10 = (f32[3,96,128]{2,1,0:T(8,128)S(1)}, f32[3,96,128]{2,1,0:T(8,128)S(1)}, u32[]{:S(2)}, u32[]{:S(2)}) collective-permute-start(f32[3,96,128]{2,1,0:T(8,128)S(1)} %get-tuple-element.31), channel_id=1, source_target_pairs={{0,1},{1,0},{2,3},{3,2},{4,5},{5,4},{6,7},{7,6},{8,9},{9,8},{10,11... | collective-permute-start | bytes 442376 | tf_op jit(solution)/shard_map/ppermute | solution.py:143
  30.0 3.3 %collective-permute-done.4.rest_2_ = f32[3,96,128]{2,1,0:T(8,128)S(1)} collective-permute-done((f32[3,96,128]{2,1,0:T(8,128)S(1)}, f32[3,96,128]{2,1,0:T(8,128)S(1)}, u32[]{:S(2)}, u32[]{:S(2)}) %collective-permute-start.4) | collective-permute-done | bytes 147488 | tf_op jit(solution)/shard_map/ppermute | solution.py:143
  33.4 1.0 %collective-permute-done.5.rest_3_ = f32[3,96,128]{2,1,0:T(8,128)S(1)} collective-permute-done((f32[3,96,128]{2,1,0:T(8,128)S(1)}, f32[3,96,128]{2,1,0:T(8,128)S(1)}, u32[]{:S(2)}, u32[]{:S(2)}) %collective-permute-start.5) | collective-permute-done | bytes 147488 | tf_op jit(solution)/shard_map/ppermute | solution.py:143
  34.4 0.0 copy-done
  34.4 0.1 offset.1.offset_ref
  34.5 0.0 collective-permute-done.8.rest_0_
  34.5 1.3 %collective-permute-done.9.rest_1_ = f32[3,96,128]{2,1,0:T(8,128)S(1)} collective-permute-done((f32[3,96,128]{2,1,0:T(8,128)S(1)}, f32[3,96,128]{2,1,0:T(8,128)S(1)}, u32[]{:S(2)}, u32[]{:S(2)}) %collective-permute-start.9) | collective-permute-done | bytes 147488 | tf_op jit(solution)/shard_map/ppermute | solution.py:143
  35.8 0.0 collective-permute-done.10.rest_2_
  35.8 0.9 %combine.1 = f32[3,96,512]{2,1,0:T(8,128)} custom-call(s32[1]{0:T(128)} %bitcast.wall_ref, f32[3,96,512]{2,1,0:T(8,128)S(1)} %offset.1.offset_ref, f32[3,96,128]{2,1,0:T(8,128)S(1)} %collective-permute-done.8.rest_0_, f32[3,96,128]{2,1,0:T(8,128)S(1)} %collective-permute-done.9.rest_1_, f32[3,96,128]{2,1,0:T(8,128)S(1)} %collective-permute-done.10.rest_2_, ...), custom_call_target="tpu_custom_call" | custom-call | flops 1000000 | bytes 3145728 | tf_op jit(solution)/shard_map/combine/pallas_call | solution.py:199
Async XLA Ops:
  0.0 14.7 %copy-start.1 = (f32[2,384,384]{2,1,0:T(8,128)S(1)}, f32[2,384,384]{2,1,0:T(8,128)}, u32[]{:S(2)}) copy-start(f32[2,384,384]{2,1,0:T(8,128)} %ops_ref.1) | copy-start | bytes 3538948
  1.3 10.3 %collective-permute-start = (f32[3,96,128]{2,1,0:T(8,128)S(1)}, f32[3,96,128]{2,1,0:T(8,128)S(1)}, u32[]{:S(2)}, u32[]{:S(2)}) collective-permute-start(f32[3,96,128]{2,1,0:T(8,128)S(1)} %get-tuple-element.35), channel_id=1, source_target_pairs={{0,28},{1,29},{2,30},{3,31},{4,0},{5,1},{6,2},{7,3},{8,4},{9,5},{1... | collective-permute-start | bytes 442376 | tf_op jit(solution)/shard_map/ppermute | solution.py:143
  7.3 7.4 %collective-permute-start.1 = (f32[3,96,128]{2,1,0:T(8,128)S(1)}, f32[3,96,128]{2,1,0:T(8,128)S(1)}, u32[]{:S(2)}, u32[]{:S(2)}) collective-permute-start(f32[3,96,128]{2,1,0:T(8,128)S(1)} %get-tuple-element.34), channel_id=1, source_target_pairs={{0,29},{1,28},{2,31},{3,30},{4,1},{5,0},{6,3},{7,2},{8,5},{9,4},{1... | collective-permute-start | bytes 442376 | tf_op jit(solution)/shard_map/ppermute | solution.py:143
  7.3 12.0 %collective-permute-start.6 = (f32[3,96,128]{2,1,0:T(8,128)S(1)}, f32[3,96,128]{2,1,0:T(8,128)S(1)}, u32[]{:S(2)}, u32[]{:S(2)}) collective-permute-start(f32[3,96,128]{2,1,0:T(8,128)S(1)} %get-tuple-element.36), channel_id=1, source_target_pairs={{0,30},{1,31},{2,28},{3,29},{4,2},{5,3},{6,0},{7,1},{8,6},{9,7},{1... | collective-permute-start | bytes 442376 | tf_op jit(solution)/shard_map/ppermute | solution.py:143
  9.3 12.2 %collective-permute-start.7 = (f32[3,96,128]{2,1,0:T(8,128)S(1)}, f32[3,96,128]{2,1,0:T(8,128)S(1)}, u32[]{:S(2)}, u32[]{:S(2)}) collective-permute-start(f32[3,96,128]{2,1,0:T(8,128)S(1)} %get-tuple-element.33), channel_id=1, source_target_pairs={{0,31},{1,30},{2,29},{3,28},{4,3},{5,2},{6,1},{7,0},{8,7},{9,6},{1... | collective-permute-start | bytes 442376 | tf_op jit(solution)/shard_map/ppermute | solution.py:143
  14.7 1.1 %copy-start.2 = (f32[1,3,384,128]{3,2,1,0:T(8,128)S(1)}, f32[1,3,384,128]{3,2,1,0:T(8,128)}, u32[]{:S(2)}) copy-start(f32[1,3,384,128]{3,2,1,0:T(8,128)} %param.7) | copy-start | bytes 1769476
  15.8 1.1 %copy-start.3 = (f32[1,3,384,128]{3,2,1,0:T(8,128)S(1)}, f32[1,3,384,128]{3,2,1,0:T(8,128)}, u32[]{:S(2)}) copy-start(f32[1,3,384,128]{3,2,1,0:T(8,128)} %param.8) | copy-start | bytes 1769476
  17.6 9.5 %collective-permute-start.2 = (f32[3,96,128]{2,1,0:T(8,128)S(1)}, f32[3,96,128]{2,1,0:T(8,128)S(1)}, u32[]{:S(2)}, u32[]{:S(2)}) collective-permute-start(f32[3,96,128]{2,1,0:T(8,128)S(1)} %get-tuple-element.20), channel_id=1, source_target_pairs={{0,7},{1,6},{2,5},{3,4},{4,11},{5,10},{6,9},{7,8},{8,15},{9,14},{1... | collective-permute-start | bytes 442376 | tf_op jit(solution)/shard_map/ppermute | solution.py:143
  18.5 10.4 %collective-permute-start.3 = (f32[3,96,128]{2,1,0:T(8,128)S(1)}, f32[3,96,128]{2,1,0:T(8,128)S(1)}, u32[]{:S(2)}, u32[]{:S(2)}) collective-permute-start(f32[3,96,128]{2,1,0:T(8,128)S(1)} %get-tuple-element.21), channel_id=1, source_target_pairs={{0,6},{1,7},{2,4},{3,5},{4,10},{5,11},{6,8},{7,9},{8,14},{9,15},{1... | collective-permute-start | bytes 442376 | tf_op jit(solution)/shard_map/ppermute | solution.py:143
  19.0 14.4 %collective-permute-start.4 = (f32[3,96,128]{2,1,0:T(8,128)S(1)}, f32[3,96,128]{2,1,0:T(8,128)S(1)}, u32[]{:S(2)}, u32[]{:S(2)}) collective-permute-start(f32[3,96,128]{2,1,0:T(8,128)S(1)} %get-tuple-element.22), channel_id=1, source_target_pairs={{0,5},{1,4},{2,7},{3,6},{4,9},{5,8},{6,11},{7,10},{8,13},{9,12},{1... | collective-permute-start | bytes 442376 | tf_op jit(solution)/shard_map/ppermute | solution.py:143
  19.3 15.1 %collective-permute-start.5 = (f32[3,96,128]{2,1,0:T(8,128)S(1)}, f32[3,96,128]{2,1,0:T(8,128)S(1)}, u32[]{:S(2)}, u32[]{:S(2)}) collective-permute-start(f32[3,96,128]{2,1,0:T(8,128)S(1)} %get-tuple-element.23), channel_id=1, source_target_pairs={{0,4},{1,5},{2,6},{3,7},{4,8},{5,9},{6,10},{7,11},{8,12},{9,13},{1... | collective-permute-start | bytes 442376 | tf_op jit(solution)/shard_map/ppermute | solution.py:143
  21.5 12.9 %copy-start = (f32[1,3,96,512]{3,2,1,0:T(8,128)S(1)}, f32[1,3,96,512]{3,2,1,0:T(8,128)}, u32[]{:S(2)}) copy-start(f32[1,3,96,512]{3,2,1,0:T(8,128)} %param.6) | copy-start | bytes 1769476
  22.9 11.6 %collective-permute-start.8 = (f32[3,96,128]{2,1,0:T(8,128)S(1)}, f32[3,96,128]{2,1,0:T(8,128)S(1)}, u32[]{:S(2)}, u32[]{:S(2)}) collective-permute-start(f32[3,96,128]{2,1,0:T(8,128)S(1)} %get-tuple-element.29), channel_id=1, source_target_pairs={{0,3},{1,2},{2,1},{3,0},{4,7},{5,6},{6,5},{7,4},{8,11},{9,10},{10,... | collective-permute-start | bytes 442376 | tf_op jit(solution)/shard_map/ppermute | solution.py:143
  27.1 8.7 %collective-permute-start.9 = (f32[3,96,128]{2,1,0:T(8,128)S(1)}, f32[3,96,128]{2,1,0:T(8,128)S(1)}, u32[]{:S(2)}, u32[]{:S(2)}) collective-permute-start(f32[3,96,128]{2,1,0:T(8,128)S(1)} %get-tuple-element.30), channel_id=1, source_target_pairs={{0,2},{1,3},{2,0},{3,1},{4,6},{5,7},{6,4},{7,5},{8,10},{9,11},{10,... | collective-permute-start | bytes 442376 | tf_op jit(solution)/shard_map/ppermute | solution.py:143
  28.9 6.9 %collective-permute-start.10 = (f32[3,96,128]{2,1,0:T(8,128)S(1)}, f32[3,96,128]{2,1,0:T(8,128)S(1)}, u32[]{:S(2)}, u32[]{:S(2)}) collective-permute-start(f32[3,96,128]{2,1,0:T(8,128)S(1)} %get-tuple-element.31), channel_id=1, source_target_pairs={{0,1},{1,0},{2,3},{3,2},{4,5},{5,4},{6,7},{7,6},{8,9},{9,8},{10,11... | collective-permute-start | bytes 442376 | tf_op jit(solution)/shard_map/ppermute | solution.py:143
